TPU v7x, 128 devices: a whole 4x4x4 slice. The times are simulated.
128 devices in a mesh: seq: 16 (over x_lo, z, core), fsdp: 8 (over y, x_hi).
Axes of the slice: x: 4 (x_hi: 2, x_lo: 2; x = x_hi * 2 + x_lo), y: 4, z: 4, core: 2. Of those that a mesh axis runs over, the one named last changes fastest.
Arguments:
- img_tokens: bfloat16 [4096, 3072], P('seq'), may hold values from -6 to 6
- txt_tokens: bfloat16 [512, 3072], P('seq'), may hold values from -6 to 6
- img_weight: bfloat16 [3072, 3, 2048], P('fsdp'), may hold values from -0.109375 to 0.109375
- txt_weight: bfloat16 [3072, 3, 2048], P('fsdp'), may hold values from -0.109375 to 0.109375
- img_modulation: bfloat16 [256, 6144], replicated, may hold values from -0.375 to 0.375
- txt_modulation: bfloat16 [256, 6144], replicated, may hold values from -0.375 to 0.375
- qk_gains: float32 [2, 2, 128], replicated, may hold values from 0.5 to 1.5
- timestep: int32 [1], replicated, may hold values from 0 to 999
- valid_text: int32 [1], replicated, may hold values from 256 to 512
- img_cotangent: bfloat16 [4096, 2048], P('seq', 'fsdp'), may hold values from -48 to 48
- txt_cotangent: bfloat16 [512, 2048], P('seq', 'fsdp'), may hold values from -48 to 48
Outputs:
- img_weight_grad: float32 [3072, 3, 2048], P('seq', None, 'fsdp')
- txt_weight_grad: float32 [3072, 3, 2048], P('seq', None, 'fsdp')
- img_input_grad: bfloat16 [4096, 3072], P('seq', 'fsdp')
- txt_input_grad: bfloat16 [512, 3072], P('seq', 'fsdp')
All inputs are finite; a program needn't handle non-finite values.
Results may differ from a plain program's by a relative error of at most 0.03.
Values may be sent and summed in bfloat16 or wider, within the bound.
A program may use at most 128 MiB of HBM per device.

v0:
```python
import math

import jax
import jax.numpy as jnp
from jax import lax
from jax.sharding import PartitionSpec as P

HD = 128


def time_features(timestep, freq_dim):
    half_freq = freq_dim // 2
    frequency = jnp.exp(-math.log(10000.0) * jnp.arange(half_freq, dtype=jnp.float32) / half_freq)
    angles = timestep.astype(jnp.float32)[:, None] * frequency[None, :]
    features = jnp.concatenate([jnp.cos(angles), jnp.sin(angles)], axis=1)
    return jax.nn.silu(features).astype(jnp.bfloat16)


def modulation(features, table, model_width):
    mixed = jnp.dot(features, table, preferred_element_type=jnp.float32)[0]
    return (mixed[:model_width], mixed[model_width:])


def prepare(tokens, shifts, scales):
    values = tokens.astype(jnp.float32)
    centred = values - jnp.mean(values, axis=-1, keepdims=True)
    inv_std = lax.rsqrt(jnp.mean(centred * centred, axis=-1, keepdims=True) + 1e-06)
    normed = centred * inv_std
    hidden = (normed * (1.0 + scales) + shifts).astype(jnp.bfloat16)
    return (hidden, normed, inv_std)


def qk_norm(values, gains):
    return values * lax.rsqrt(jnp.mean(values * values, axis=-1, keepdims=True) + 1e-06) * gains


def norm_grads(q_pre, k_pre, gains, grad_q, grad_k):

    def normalize(query_pre, key_pre):
        return (qk_norm(query_pre, gains[0]), qk_norm(key_pre, gains[1]))

    outputs, pullback = jax.vjp(normalize, q_pre, k_pre)
    return pullback((grad_q, grad_k))


def input_grad(grad_hidden, scales, normed, inv_std):
    scaled = grad_hidden * (1.0 + scales)
    mean_grad = jnp.mean(scaled, axis=-1, keepdims=True)
    mean_cross = jnp.mean(scaled * normed, axis=-1, keepdims=True)
    return (inv_std * (scaled - mean_grad - normed * mean_cross)).astype(jnp.bfloat16)


def on_device(
    img_tokens,
    txt_tokens,
    img_weight,
    txt_weight,
    img_modulation,
    txt_modulation,
    qk_gains,
    timestep,
    valid_text,
    img_cotangent,
    txt_cotangent,
):
    model_width = img_tokens.shape[1]
    txt_rows = txt_tokens.shape[0]
    img_rows = img_tokens.shape[0]
    all_rows = txt_rows + img_rows
    col_width = img_cotangent.shape[1]
    group_heads = col_width // HD
    seq_devices = lax.axis_size("seq")
    fsdp_devices = lax.axis_size("fsdp")
    key_count = all_rows * seq_devices
    score_scale = HD ** (-0.5)
    share = model_width // fsdp_devices
    col_offset = lax.axis_index("fsdp") * share
    features = time_features(timestep, img_modulation.shape[0])
    prepared = []
    for tokens, table in ((txt_tokens, txt_modulation), (img_tokens, img_modulation)):
        shifts, scales = modulation(features, table, model_width)
        hidden, normed, inv_std = prepare(tokens, shifts, scales)
        prepared.append((hidden, normed, inv_std, scales))
    txt_block, img_block = (
        lax.all_to_all(txt_weight, "fsdp", split_axis=2, concat_axis=0, tiled=True),
        lax.all_to_all(img_weight, "fsdp", split_axis=2, concat_axis=0, tiled=True),
    )
    flat_blocks = (
        txt_block.reshape(model_width, 3 * col_width),
        img_block.reshape(model_width, 3 * col_width),
    )
    qkv_list = tuple(
        (
            jnp.dot(prepared[which][0], flat_blocks[which], preferred_element_type=jnp.float32)
            for which in range(2)
        )
    )
    streams = []
    for which in range(2):
        hidden, normed, inv_std, scales = prepared[which]
        streams.append(
            (
                hidden,
                normed,
                inv_std,
                scales,
                qkv_list[which].reshape(-1, 3, group_heads, HD),
                flat_blocks[which],
            )
        )
    query = jnp.concatenate(
        [qk_norm(streams[which][4][:, 0], qk_gains[which, 0]) for which in range(2)], 0
    ).astype(jnp.bfloat16)
    keys_own = jnp.concatenate(
        [qk_norm(streams[which][4][:, 1], qk_gains[which, 1]) for which in range(2)], 0
    ).astype(jnp.bfloat16)
    values_own = jnp.concatenate([streams[which][4][:, 2] for which in range(2)], 0).astype(
        jnp.bfloat16
    )

    def live_keys(amount):
        positions = jnp.arange(amount, dtype=jnp.int32)
        in_shard = positions % all_rows
        text_index = positions // all_rows * txt_rows + in_shard
        return ((in_shard >= txt_rows) | (text_index < valid_text[0])).astype(jnp.float32)

    key_block = lax.all_gather(keys_own, "seq", axis=0, tiled=True)
    value_block = lax.all_gather(values_own, "seq", axis=0, tiled=True)
    scores = (
        jnp.einsum("qgd,kgd->gqk", query, key_block, preferred_element_type=jnp.float32)
        * score_scale
    )
    expo = jnp.exp(scores) * live_keys(key_block.shape[0])[None, None, :]
    summed = jnp.einsum(
        "gqk,kgd->qgd", expo.astype(jnp.bfloat16), value_block, preferred_element_type=jnp.float32
    )
    totals = jnp.sum(expo, axis=-1).T
    key_whole, value_whole = (
        lax.all_gather(keys_own, "seq", axis=0, tiled=True),
        lax.all_gather(values_own, "seq", axis=0, tiled=True),
    )
    attended = (summed / totals[..., None]).astype(jnp.bfloat16)
    grad_out = jnp.concatenate([txt_cotangent, img_cotangent], 0).reshape(all_rows, group_heads, HD)
    deltas = jnp.sum(grad_out.astype(jnp.float32) * attended.astype(jnp.float32), axis=-1)
    scores = (
        jnp.einsum("qgd,kgd->gqk", query, key_whole, preferred_element_type=jnp.float32)
        * score_scale
    )
    attn_probs = jnp.exp(scores) * live_keys(key_count)[None, None, :] / totals.T[:, :, None]
    grad_probs = jnp.einsum(
        "qgd,kgd->gqk", grad_out, value_whole, preferred_element_type=jnp.float32
    )
    grad_scores = (attn_probs * (grad_probs - deltas.T[:, :, None])).astype(jnp.bfloat16)
    grad_q = (
        jnp.einsum("gqk,kgd->qgd", grad_scores, key_whole, preferred_element_type=jnp.float32)
        * score_scale
    )
    probs_low = attn_probs.astype(jnp.bfloat16)
    grad_k_part = (
        jnp.einsum("gqk,qgd->kgd", grad_scores, query, preferred_element_type=jnp.float32)
        * score_scale
    )
    grad_v_part = jnp.einsum(
        "gqk,qgd->kgd", probs_low, grad_out, preferred_element_type=jnp.float32
    )
    summed_keys = lax.psum_scatter(
        jnp.stack([grad_k_part, grad_v_part], 1).astype(jnp.bfloat16),
        "seq",
        scatter_dimension=0,
        tiled=True,
    ).astype(jnp.float32)
    grad_k, grad_v = (summed_keys[:, 0], summed_keys[:, 1])
    bounds = ((0, txt_rows), (txt_rows, all_rows))
    grad_flat = []
    for which in range(2):
        qkv = streams[which][4]
        row_begin, row_end = bounds[which]
        grad_q_pre, grad_k_pre = norm_grads(
            qkv[:, 0],
            qkv[:, 1],
            qk_gains[which],
            grad_q[row_begin:row_end],
            grad_k[row_begin:row_end],
        )
        grad_qkv = jnp.stack([grad_q_pre, grad_k_pre, grad_v[row_begin:row_end]], 1).astype(
            jnp.bfloat16
        )
        grad_flat.append(grad_qkv.reshape(-1, 3 * col_width))

    def weight_terms():
        parts = [
            jnp.einsum(
                "nc,nw->cw", streams[which][0], grad_flat[which], preferred_element_type=jnp.float32
            )
            for which in range(2)
        ]
        return jnp.stack(parts, 1)

    weight_sum = lax.psum_scatter(
        weight_terms().astype(jnp.bfloat16), "seq", scatter_dimension=0, tiled=True
    ).astype(jnp.float32)
    txt_weight_grad = weight_sum[:, 0].reshape(-1, 3, col_width)
    img_weight_grad = weight_sum[:, 1].reshape(-1, 3, col_width)
    scale_rows = jnp.concatenate(
        [
            jnp.broadcast_to(streams[0][3], (txt_rows, model_width)),
            jnp.broadcast_to(streams[1][3], (img_rows, model_width)),
        ],
        0,
    )
    normed_all = jnp.concatenate([streams[0][1], streams[1][1]], 0)
    inv_all = jnp.concatenate([streams[0][2], streams[1][2]], 0)
    hidden_part = jnp.concatenate(
        [
            jnp.einsum(
                "nw,dw->nd", grad_flat[which], streams[which][5], preferred_element_type=jnp.float32
            )
            for which in range(2)
        ],
        0,
    )
    grad_whole = lax.psum(hidden_part.astype(jnp.bfloat16), "fsdp").astype(jnp.float32)
    full_grads = input_grad(grad_whole, scale_rows, normed_all, inv_all)
    input_grads = lax.dynamic_slice_in_dim(full_grads, col_offset, share, 1)
    return (img_weight_grad, txt_weight_grad, input_grads[txt_rows:], input_grads[:txt_rows])


def solution(mesh):
    return jax.shard_map(
        on_device,
        mesh=mesh,
        in_specs=(
            P("seq", None),
            P("seq", None),
            P("fsdp", None, None),
            P("fsdp", None, None),
            P(),
            P(),
            P(),
            P(),
            P(),
            P("seq", "fsdp"),
            P("seq", "fsdp"),
        ),
        out_specs=(
            P("seq", None, "fsdp"),
            P("seq", None, "fsdp"),
            P("seq", "fsdp"),
            P("seq", "fsdp"),
        ),
        check_vma=False,
    )
```

profile of v0, /device:TPU:1, one launch (start us, length us, event | category | flops | bytes accessed | tf_op | source)
XLA Modules:
  0.0 546.0 jit_solution(13137071091209567767)
XLA Ops:
  7.2 10.4 %copy.33 = bf16[384,3,2048]{0,1,2:T(4,128)(2,1)} copy(bf16[384,3,2048]{2,0,1:T(8,128)(2,1)} %param.14) | data formatting | bytes 9437184 | tf_op args[3]
  17.6 7.5 %all-to-all-start = ((bf16[384,3,2048]{0,1,2:T(4,128)(2,1)}), bf16[384,3,2048]{0,1,2:T(4,128)(2,1)}, u32[]{:S(2)}, u32[]{:S(2)}) async-start(bf16[384,3,2048]{0,1,2:T(4,128)(2,1)} %copy.33), calls=%async_computation | async-start | bytes 12582912 | tf_op jit(solution)/shard_map/all_to_all | solution.py:85
  25.1 10.3 %copy.35 = bf16[384,3,2048]{0,1,2:T(4,128)(2,1)} copy(bf16[384,3,2048]{2,0,1:T(8,128)(2,1)} %param.13) | data formatting | bytes 9437184 | tf_op args[2]
  35.5 62.2 %all-to-all-done = bf16[384,3,2048]{0,1,2:T(4,128)(2,1)} async-done(((bf16[384,3,2048]{0,1,2:T(4,128)(2,1)}), bf16[384,3,2048]{0,1,2:T(4,128)(2,1)}, u32[]{:S(2)}, u32[]{:S(2)}) %all-to-all-start) | async-done | bytes 4718624 | tf_op jit(solution)/shard_map/all_to_all | solution.py:85
  97.7 4.8 all-to-all-start.1
  103.6 0.2 fusion.42
  103.8 1.7 convert_reduce_fusion
  105.5 2.0 fusion.13
  107.6 0.5 fusion.93
  108.1 0.6 fusion.90
  108.7 0.5 fusion.94
  109.2 6.4 %copy.34 = bf16[8,384,3,256]{1,0,3,2:T(8,128)(2,1)S(1)} copy(bf16[8,384,3,256]{1,2,3,0:T(4,128)(2,1)} %bitcast.5) | data formatting | bytes 9437184 | tf_op jit(solution)/shard_map/all_to_all | solution.py:85
  115.6 1.2 copy.51
  116.8 2.2 copy-done.4
  119.0 1.5 fusion.49
  120.6 53.4 %all-to-all-done.1 = bf16[384,3,2048]{0,1,2:T(4,128)(2,1)} async-done(((bf16[384,3,2048]{0,1,2:T(4,128)(2,1)}), bf16[384,3,2048]{0,1,2:T(4,128)(2,1)}, u32[]{:S(2)}, u32[]{:S(2)}) %all-to-all-start.1) | async-done | bytes 4718624 | tf_op jit(solution)/shard_map/all_to_all | solution.py:86
  174.0 6.4 %copy.36 = bf16[8,384,3,256]{1,0,3,2:T(8,128)(2,1)S(1)} copy(bf16[8,384,3,256]{1,2,3,0:T(4,128)(2,1)} %bitcast.14) | data formatting | bytes 9437184 | tf_op jit(solution)/shard_map/all_to_all | solution.py:86
  180.4 1.3 copy.52
  181.8 1.7 fusion.14
  183.5 0.4 copy-done.6
  184.5 0.7 pad_maximum_fusion.5
  185.3 0.7 pad_maximum_fusion.6
  186.7 34.0 %all-gather.3.cloned.1.call-done = bf16[4608,2,128]{2,0,1:T(8,128)(2,1)} async-done(((bf16[288,2,128]{2,0,1:T(8,128)(2,1)}), bf16[4608,2,128]{2,0,1:T(8,128)(2,1)}) %all-gather.3.cloned.1.call-update) | async-done | bytes 2359312 | tf_op jit(solution)/shard_map/all_gather | solution.py:139
  220.7 3.9 fusion.92
  224.6 4.0 copy-done.2
  228.6 4.1 fusion.1
  232.8 24.6 %all-gather.5.cloned.1.call-done = bf16[4608,2,128]{2,0,1:T(8,128)(2,1)} async-done(((bf16[288,2,128]{2,0,1:T(8,128)(2,1)}), bf16[4608,2,128]{2,0,1:T(8,128)(2,1)}) %all-gather.5.cloned.1.call-update) | async-done | bytes 2359312 | tf_op jit(solution)/shard_map/all_gather | solution.py:140
  257.4 6.5 %fusion.32 = f32[288,2]{0,1:T(2,128)S(1)} fusion(bf16[4608,2,128]{2,0,1:T(8,128)(2,1)} %all-gather.5.cloned.1.call-done, f32[2,288,4608]{2,1,0:T(8,128)} %copy-done.2, f32[288,2]{0,1:T(2,128)S(1)} %bitcast.184, bf16[256,256]{1,0:T(8,128)(2,1)S(1)} %copy-done.17, bf16[32,256]{1,0:T(8,128)(2,1)S(1)} %copy-done.18), kind=kOutput, calls=%fused_computation.42 | convolution fusion | flops 682868160 | bytes 13128192 | tf_op jit(solution)/shard_map/gqk,kgd->qgd/dot_general | solution.py:134
  263.9 1.2 copy-done.3
  265.1 0.7 copy-done.13
  265.8 1.9 multiply_convert_fusion
  267.7 3.0 fusion.2
  270.7 0.4 copy-done.15
  271.1 2.6 pad_maximum_fusion.2
  273.7 0.3 all-reduce.2.cloned.1.call-start
  274.0 4.8 fusion.19
  278.7 58.4 %reduce-scatter.3.cloned.1.call-done = bf16[288,2,2,128]{3,0,2,1:T(8,128)(2,1)} async-done(((bf16[4608,2,2,128]{3,0,2,1:T(8,128)(2,1)}), bf16[288,2,2,128]{3,0,2,1:T(8,128)(2,1)}) %reduce-scatter.3.cloned.1.call-update) | async-done | bytes 294928 | tf_op jit(solution)/shard_map/reduce_scatter | solution.py:166
  337.2 1.0 convert_element_type.107
  338.7 0.3 copy-done.14
  339.1 0.7 slice.146
  340.2 1.2 add_add_fusion
  341.3 0.9 slice.149
  342.3 0.9 copy.43
  343.2 3.3 convolution_convert_fusion.4
  346.5 3.8 convolution_convert_fusion.3
  350.3 1.4 pad_maximum_fusion.3
  351.7 3.6 fusion.6
  355.4 4.1 fusion.7
  359.5 8.3 %pad_maximum_fusion = bf16[3072,2,768]{2,0,1:T(8,128)(2,1)} fusion(bf16[3072,1,768]{2,0,1:T(8,128)(2,1)} %fusion.7, bf16[3072,1,768]{2,0,1:T(8,128)(2,1)} %fusion.6), kind=kLoop, calls=%fused_computation.2 | loop fusion | flops 4718592 | bytes 18874368 | tf_op jit(solution)/shard_map/stack | solution.py:197
  367.8 0.7 maximum_reduce_fusion
  368.5 0.8 fusion.35
  369.3 2.0 fusion.8
  371.4 79.3 %all-reduce.2.cloned.1.call-done = bf16[288,3072]{1,0:T(8,128)(2,1)} async-done(((bf16[288,3072]{1,0:T(8,128)(2,1)}), bf16[288,3072]{1,0:T(8,128)(2,1)}) %all-reduce.2.cloned.1.call-update) | async-done | bytes 1769488 | tf_op jit(solution)/shard_map/psum | solution.py:222
  450.7 0.3 broadcast_in_dim.17
  451.0 0.9 broadcast_in_dim.16
  452.1 0.9 fusion.86
  453.3 0.7 slice.152
  454.0 0.6 slice.153
  454.6 74.1 %reduce-scatter.5.cloned.1.call-done = bf16[192,2,768]{2,0,1:T(8,128)(2,1)} async-done(((bf16[3072,2,768]{2,0,1:T(8,128)(2,1)}), bf16[192,2,768]{2,0,1:T(8,128)(2,1)}) %reduce-scatter.5.cloned.1.call-update) | async-done | bytes 589840 | tf_op jit(solution)/shard_map/reduce_scatter | solution.py:199
  528.7 2.1 fusion.89
  530.8 2.2 reshape_squeeze.6
  533.1 2.1 copy.44
  535.1 2.2 reshape_squeeze.7
  537.4 2.1 copy.45
  (83 shorter events, 2.6 us)
Async XLA Ops:
  7.2 100.4 %copy-start = (bf16[256,6144]{1,0:T(8,128)(2,1)S(1)}, bf16[256,6144]{1,0:T(8,128)(2,1)}, u32[]{:S(2)}) copy-start(bf16[256,6144]{1,0:T(8,128)(2,1)} %param.16) | copy-start | bytes 9437188
  17.6 80.1 %all-to-all-start = ((bf16[384,3,2048]{0,1,2:T(4,128)(2,1)}), bf16[384,3,2048]{0,1,2:T(4,128)(2,1)}, u32[]{:S(2)}, u32[]{:S(2)}) async-start(bf16[384,3,2048]{0,1,2:T(4,128)(2,1)} %copy.33), calls=%async_computation | async-start | bytes 12582912 | tf_op jit(solution)/shard_map/all_to_all | solution.py:85
  35.4 68.0 %copy-start.8 = (bf16[32,3072]{1,0:T(8,128)(2,1)S(1)}, bf16[32,3072]{1,0:T(8,128)(2,1)}, u32[]{:S(2)}) copy-start(bf16[32,3072]{1,0:T(8,128)(2,1)} %param.12) | copy-start | bytes 589828
  97.7 76.3 %all-to-all-start.1 = ((bf16[384,3,2048]{0,1,2:T(4,128)(2,1)}), bf16[384,3,2048]{0,1,2:T(4,128)(2,1)}, u32[]{:S(2)}, u32[]{:S(2)}) async-start(bf16[384,3,2048]{0,1,2:T(4,128)(2,1)} %copy.35), calls=%async_computation.1 | async-start | bytes 12582912 | tf_op jit(solution)/shard_map/all_to_all | solution.py:86
  102.5 5.0 copy-start.21
  102.5 118.2 %all-gather.3.cloned.1.call-start = ((), (), s32[]{:S(2)}) async-start(), calls=%async_computation.4 | async-start | bytes 2506752 | tf_op jit(solution)/shard_map/all_gather | solution.py:139
  102.5 6.2 %copy-start.10 = (bf16[256,6144]{1,0:T(8,128)(2,1)S(1)}, bf16[256,6144]{1,0:T(8,128)(2,1)}, u32[]{:S(2)}) copy-start(bf16[256,6144]{1,0:T(8,128)(2,1)} %param.15) | copy-start | bytes 9437188
  107.5 260.3 %copy-start.19 = (f32[256]{0:T(256)}, f32[256]{0:T(256)S(1)}, u32[]{:S(2)}) copy-start(f32[256]{0:T(256)S(1)} %add_rsqrt_fusion) | copy-start | bytes 3076
  116.8 2.2 copy-start.4
  180.4 1.4 copy-start.7
  181.7 2.2 copy-start.6
  185.2 72.2 %all-gather.5.cloned.1.call-start = ((), (), s32[]{:S(2)}) async-start(), calls=%async_computation.5 | async-start | bytes 2506752 | tf_op jit(solution)/shard_map/all_gather | solution.py:140
  186.0 151.2 %reduce-scatter.3.cloned.1.call-start = ((), (), s32[]{:S(2)}) async-start(), calls=%async_computation.6 | async-start | bytes 5013504 | tf_op jit(solution)/shard_map/reduce_scatter | solution.py:166
  220.7 7.9 %copy-start.17 = (bf16[256,256]{1,0:T(8,128)(2,1)S(1)}, bf16[256,256]{1,0:T(8,128)(2,1)}, u32[]{:S(2)}) copy-start(bf16[256,256]{1,0:T(8,128)(2,1)} %param.20) | copy-start | bytes 393220
  220.7 7.9 %copy-start.18 = (bf16[32,256]{1,0:T(8,128)(2,1)S(1)}, bf16[32,256]{1,0:T(8,128)(2,1)}, u32[]{:S(2)}) copy-start(bf16[32,256]{1,0:T(8,128)(2,1)} %param.21) | copy-start | bytes 49156
  224.6 4.0 copy-start.2
  257.4 7.7 %copy-start.3 = (f32[2,288,4608]{2,1,0:T(8,128)S(1)}, f32[2,288,4608]{2,1,0:T(8,128)}, u32[]{:S(2)}) copy-start(f32[2,288,4608]{2,1,0:T(8,128)} %copy-done.2) | copy-start | bytes 31850500
  257.4 8.4 %copy-start.13 = (bf16[4608,2,128]{2,0,1:T(8,128)(2,1)S(1)}, bf16[4608,2,128]{2,0,1:T(8,128)(2,1)}, u32[]{:S(2)}) copy-start(bf16[4608,2,128]{2,0,1:T(8,128)(2,1)} %all-gather.5.cloned.1.call-done) | copy-start | bytes 7077892
  267.6 3.1 copy-start.5
  267.6 3.4 copy-start.15
  273.7 177.0 %all-reduce.2.cloned.1.call-start = ((), (), s32[]{:S(2)}) async-start(), calls=%async_computation.8 | async-start | bytes 3538944 | tf_op jit(solution)/shard_map/psum | solution.py:222
  338.2 0.8 copy-start.14
  343.2 3.3 copy-start.11
  351.7 3.7 copy-start.12
  351.7 177.0 %reduce-scatter.5.cloned.1.call-start = ((), (), s32[]{:S(2)}) async-start(), calls=%async_computation.7 | async-start | bytes 10027008 | tf_op jit(solution)/shard_map/reduce_scatter | solution.py:199
  369.3 82.6 %copy-start.9 = (f32[32,3072]{1,0:T(8,128)S(1)}, f32[32,3072]{1,0:T(8,128)}, u32[]{:S(2)}) copy-start(f32[32,3072]{1,0:T(8,128)} %fusion.35) | copy-start | bytes 1179652
  450.7 1.5 copy-start.16
  452.1 0.9 copy-start.20
  454.0 85.5 %copy-start.1 = (bf16[256,6144]{1,0:T(8,128)(2,1)S(1)}, bf16[256,6144]{1,0:T(8,128)(2,1)}, u32[]{:S(2)}) copy-start(bf16[256,6144]{1,0:T(8,128)(2,1)} %param.16) | copy-start | bytes 9437188
Sparse Core Ops, SparseCore 0:
  185.3 35.3 all-gather.2
  222.9 34.4 all-gather.4
  273.8 63.3 reduce-scatter.2
  351.8 98.8 all-reduce.1
  452.9 75.7 reduce-scatter.4
where the time goes:
time: 550 us; the launch traced here: 546 us
  waiting for transfers between devices  386 us (70%)
  local copies, waits for them, and re-layouts  61.6 us (11%)
  matrix products  43.3 us (8%)
  other arithmetic  26.6 us (5%)
  between operations  15.7 us (3%)
  starting transfers between devices  12.7 us (2%)
    psum x1, waiting for transfers between devices, on_device(): lax.psum(hidden_part.astype(jnp.bfloat16), 'fsdp').astype(jnp.float32)  79.3 us
    reduce_scatter x1, waiting for transfers between devices, on_device(): lax.psum_scatter(weight_terms().astype(jnp.bfloat16), 'seq', scatter_dime...  74.1 us
    all_to_all x1, waiting for transfers between devices, on_device(): lax.all_to_all(txt_weight, 'fsdp', split_axis=2, concat_axis=0, tiled=True)  62.2 us
    reduce_scatter x1, waiting for transfers between devices, on_device(): lax.psum_scatter(jnp.stack([grad_k_part, grad_v_part], 1).astype(jnp.bflo...  58.4 us
    all_to_all x1, waiting for transfers between devices, on_device(): lax.all_to_all(img_weight, 'fsdp', split_axis=2, concat_axis=0, tiled=True)  53.4 us
    unnamed x50, local copies, waits for them, and re-layouts  36.9 us
    all_gather x1, waiting for transfers between devices, on_device(): lax.all_gather(keys_own, 'seq', axis=0, tiled=True)  34 us
    all_gather x1, waiting for transfers between devices, on_device(): lax.all_gather(values_own, 'seq', axis=0, tiled=True)  24.6 us
  transfers between devices with their start and end apart: 7, of which 7 were waited for; matrix products, arithmetic and copies ran while one was open for 11% of the time, Pallas kernels for 0%

commit v1 on v0

v1 whole, which is shorter than its diff:
```python
import functools
import math

import jax
import jax.numpy as jnp
from jax import lax
from jax.experimental import pallas as pl
from jax.experimental.pallas import tpu as pltpu
from jax.sharding import PartitionSpec as P

HD = 128
BF = jnp.bfloat16
F32 = jnp.float32
MESH = pl.DeviceIdType.MESH
SCALE = HD ** (-0.5)
EXP2 = SCALE / math.log(2.0)
EPS = 1e-06


def time_features(timestep, freq_dim):
    half_freq = freq_dim // 2
    frequency = jnp.exp(-math.log(10000.0) * jnp.arange(half_freq, dtype=jnp.float32) / half_freq)
    angles = timestep.astype(jnp.float32)[:, None] * frequency[None, :]
    features = jnp.concatenate([jnp.cos(angles), jnp.sin(angles)], axis=1)
    return jax.nn.silu(features).astype(jnp.bfloat16)


def dot(a, b):
    return jnp.dot(a, b, preferred_element_type=F32)


def dot_nt(a, b):
    return lax.dot_general(a, b, (((1,), (1,)), ((), ())), preferred_element_type=F32)


def dot_tn(a, b):
    return lax.dot_general(a, b, (((0,), (0,)), ((), ())), preferred_element_type=F32)


def norm_back(x, gain, grad):
    r = lax.rsqrt(jnp.mean(x * x, axis=-1, keepdims=True) + EPS)
    gd = gain * grad
    return r * gd - x * (r * r * r * jnp.mean(x * gd, axis=-1, keepdims=True))


def kernel(
    x_img, x_txt, w_img, w_txt, mod_img, mod_txt, feat, gains, live, cot_img, cot_txt,
    dw_img, dw_txt, dx_img, dx_txt,
    xi, xt, mods, mixed, sc, W, wt, hid, hidt, htg, nimg, ntxt, invi, invt,
    tps, tpr, qkvp, dO, qT, dOT, q2, dO2, kv, kvt, ets, dkvs, dkvr, dkvts, dkvtr,
    oT, tot, gq, gtf, gts, dws, dwr, pxs, pxr, phs, phr, s1v, s2v, sts, str_,
    thx, thr, tsts, tstr, wx, wxr, wxt, wxtr, wsum,
    lsem, wl_sem, wtl_sem, w_ss, w_rs, p_ss, p_rs, t_ss, t_rs, h_ss, h_rs,
    kv_ss, kv_rs, kt_ss, kt_rs, dk_ss, dk_rs, dt_ss, dt_rs, gf_ss, gf_rs, gs_ss, gs_rs,
    dw_ss, dw_rs, ph_ss, ph_rs, st_ss, st_rs, ts_ss, ts_rs,
):
    s = lax.axis_index("seq")
    f = lax.axis_index("fsdp")
    chip, c = s // 2, s % 2
    xlo, z = chip // 4, chip % 4
    y, xhi = f // 2, f % 2
    o = 1 - c

    def f_at(r, sign):
        return ((y + sign * (r % 4) + 4) % 4) * 2 + (xhi + r // 4) % 2

    def chip_at(r, sign):
        return ((xlo + r // 4) % 2) * 4 + (z + sign * (r % 4) + 4) % 4

    def fdev(r, sign):
        return (s, f_at(r, sign))

    def sdev(r, sign):
        return (chip_at(r, sign) * 2 + c, f)

    pdev = (chip * 2 + o, f)

    def remote(src, dst, ss, rs, dev):
        return pltpu.make_async_remote_copy(
            src_ref=src, dst_ref=dst, send_sem=ss, recv_sem=rs, device_id=dev, device_id_type=MESH
        )

    def loop(lo, hi, body):
        def step(i, carry):
            body(i)
            return carry

        lax.fori_loop(lo, hi, step, 0)

    def m128(v):
        return pl.multiple_of(v, 128)

    loc = [
        pltpu.make_async_copy(x_img, xi, lsem.at[0]),
        pltpu.make_async_copy(x_txt, xt, lsem.at[1]),
        pltpu.make_async_copy(mod_img, mods.at[1], lsem.at[2]),
        pltpu.make_async_copy(mod_txt, mods.at[0], lsem.at[3]),
        pltpu.make_async_copy(
            cot_img.at[:, pl.ds(m128(c * 128), 128)],
            dO.at[pl.ds(pl.multiple_of(128 + c * 256, 128), 256)], lsem.at[4]),
        pltpu.make_async_copy(
            cot_txt.at[:, pl.ds(m128(c * 128), 128)],
            dO.at[pl.ds(pl.multiple_of(c * 32, 32), 32)], lsem.at[5]),
    ]
    for cp in loc:
        cp.start()

    barrier = pltpu.get_barrier_semaphore()

    def hello(r):
        pl.semaphore_signal(barrier, inc=1, device_id=fdev(r, 1), device_id_type=MESH)
        pl.semaphore_signal(barrier, inc=1, device_id=sdev(r, 1), device_id_type=MESH)

    loop(1, 8, hello)
    pl.semaphore_signal(barrier, inc=1, device_id=pdev, device_id_type=MESH)

    def w_cols(ref, j, fp):
        return ref.at[j, :, pl.ds(m128((2 * fp + c) * 128), 128)]

    def wl_copy(j):
        return pltpu.make_async_copy(
            w_cols(w_img, j, f), W.at[0, :, pl.ds(j * 128, 128)], wl_sem.at[j])

    def wt_copy(r, j):
        return pltpu.make_async_copy(
            w_cols(w_txt, j, f_at(r, 1)), wt.at[r, :, pl.ds(j * 128, 128)], wtl_sem.at[r, j])

    for j in range(3):
        wl_copy(j).start()

    pl.semaphore_wait(barrier, 15)

    def w_copy(r, j):
        return remote(
            w_cols(w_img, j, f_at(r, 1)), W.at[r, :, pl.ds(j * 128, 128)],
            w_ss.at[r, j], w_rs.at[r, j], fdev(r, 1))

    def send_w(r):
        for j in range(3):
            w_copy(r, j).start()

    loop(1, 8, send_w)

    def start_wt(r):
        for j in range(3):
            wt_copy(r, j).start()

    loop(0, 8, start_wt)

    img_rows = pl.ds(pl.multiple_of(128 + c * 256, 128), 256)
    txt_rows = pl.ds(pl.multiple_of(c * 32, 32), 32)
    half_rows = pl.ds(pl.multiple_of(c * 256, 256), 256)
    cp_coti = remote(cot_img.at[:, pl.ds(m128(o * 128), 128)], dO.at[img_rows],
                     p_ss.at[0], p_rs.at[0], pdev)
    cp_cott = remote(cot_txt.at[:, pl.ds(m128(o * 128), 128)], dO.at[txt_rows],
                     p_ss.at[1], p_rs.at[1], pdev)
    cp_coti.start()
    cp_cott.start()

    for which in (0, 1):
        loc[3 - which].wait()
        mixed[which] = dot(feat[...], mods[which])[:8]
        for b in range(8):
            sc[which, b] = 1.0 + mixed[which, :, 3072 + b * 384:3072 + (b + 1) * 384]

    def prepare(which, src, nrm, inv, put):
        rows = 16

        def body(i):
            at = pl.multiple_of(i * rows, rows)
            v = src[pl.ds(at, rows), :].astype(F32)
            cen = v - jnp.mean(v, axis=-1, keepdims=True)
            iv = lax.rsqrt(jnp.mean(cen * cen, axis=-1, keepdims=True) + EPS)
            n = cen * iv
            inv[pl.ds(at, rows), :] = jnp.broadcast_to(iv, (rows, 128))
            h = (n * (1.0 + mixed[which, 0:1, 3072:]) + mixed[which, 0:1, :3072]).astype(BF)
            for b in range(8):
                nrm[b, pl.ds(at, rows), :] = n[:, b * 384:(b + 1) * 384]
                put(b, at, rows, h[:, b * 384:(b + 1) * 384])

        loop(0, src.shape[0] // rows, body)

    def put_txt(b, at, rows, h):
        hidt[b, pl.ds(pl.multiple_of(c * 32 + at, 16), rows), :] = h

    def put_img(b, at, rows, h):
        hid[b, pl.ds(pl.multiple_of(c * 256 + at, 16), rows), :] = h

    loc[1].wait()
    prepare(0, xt, ntxt, invt, put_txt)
    cp_ht = remote(hidt.at[:, txt_rows], hidt.at[:, txt_rows], p_ss.at[2], p_rs.at[2], pdev)
    cp_ht.start()
    loc[0].wait()
    prepare(1, xi, nimg, invi, put_img)
    cp_hi = remote(hid.at[:, half_rows], hid.at[:, half_rows], p_ss.at[3], p_rs.at[3], pdev)
    cp_hi.start()

    cp_ht.wait_recv()

    def t_copy(r):
        return remote(tps.at[r], tpr.at[r], t_ss.at[r], t_rs.at[r], fdev(r, 1))

    def h_copy(r):
        return remote(hidt.at[chip_at(r, 1)], htg.at[r], h_ss.at[r], h_rs.at[r], sdev(r, 1))

    def txt_partial(i):
        r = (i + 1) % 8
        for j in range(3):
            wt_copy(r, j).wait()
        tps[r] = dot(hidt[f], wt[r]).astype(BF)

        @pl.when(r != 0)
        def _():
            t_copy(r).start()

    loop(0, 8, txt_partial)
    htg[0] = hidt[chip]
    loop(1, 8, lambda r: h_copy(r).start())

    loc[4].wait()
    loc[5].wait()
    cp_coti.wait_recv()
    cp_cott.wait_recv()
    dO[64:128, :] = jnp.zeros((64, 128), BF)
    dOT[...] = dO[...].astype(F32).T.astype(BF)

    cp_hi.wait_recv()
    for j in range(3):
        wl_copy(j).wait()
    qkvp[128:, :] = dot(hid[f], W[0])

    def img_proj(r):
        for j in range(3):
            w_copy(r, j).wait_recv()
        qkvp[128:, :] += dot(hid[f_at(r, -1)], W[r])

    loop(1, 8, img_proj)

    qkvp[0:64, :] = tps[0].astype(F32)
    qkvp[64:128, :] = jnp.zeros((64, 384), F32)

    def txt_add(r):
        t_copy(r).wait_recv()
        qkvp[0:64, :] += tpr[r].astype(F32)

    loop(1, 8, txt_add)

    def normed_heads(lo, hi, g0):
        a = qkvp[lo:hi, 0:128]
        b = qkvp[lo:hi, 128:256]
        qn = a * lax.rsqrt(jnp.mean(a * a, axis=-1, keepdims=True) + EPS) * gains[g0:g0 + 1, :]
        kn = b * lax.rsqrt(jnp.mean(b * b, axis=-1, keepdims=True) + EPS) * gains[g0 + 1:g0 + 2, :]
        qT[:, lo:hi] = qn.T.astype(BF)
        return kn.astype(BF)

    kv[0, :, 0:128] = normed_heads(128, 640, 2)
    kv[0, :, 128:256] = qkvp[128:, 256:384].astype(BF)

    def kv_copy(r):
        return remote(kv.at[0], kv.at[r], kv_ss.at[r], kv_rs.at[r], sdev(r, 1))

    def kt_copy(r):
        return remote(kvt.at[0], kvt.at[r], kt_ss.at[r], kt_rs.at[r], sdev(r, 1))

    loop(1, 8, lambda r: kv_copy(r).start())
    kt = normed_heads(0, 128, 0)
    kvt[0, :, 0:128] = kt[0:64]
    kvt[0, :, 128:256] = qkvp[0:64, 256:384].astype(BF)
    loop(1, 8, lambda r: kt_copy(r).start())

    oT[...] = jnp.zeros_like(oT)
    tot[...] = jnp.zeros_like(tot)

    def forward(r):
        @pl.when(r != 0)
        def _():
            kv_copy(r).wait_recv()

        e = jnp.exp2(dot(kv[r, :, 0:128], qT[...]) * EXP2)
        tot[0:1, :] += jnp.sum(e, axis=0, keepdims=True)
        eb = e.astype(BF)
        ets[r] = eb
        oT[...] += dot_tn(kv[r, :, 128:256], eb)

    loop(0, 8, forward)
    loop(1, 8, lambda r: kt_copy(r).wait_recv())

    def forward_text(r):
        rows = pl.ds(pl.multiple_of(r * 64, 64), 64)
        e = jnp.exp2(dot(kvt[r, :, 0:128], qT[...]) * EXP2)
        e = e * live[pl.ds(pl.multiple_of(chip_at(r, -1) * 64, 64), 64), 0:1]
        tot[0:1, :] += jnp.sum(e, axis=0, keepdims=True)
        ets[8, rows, :] = e.astype(BF)

    loop(0, 8, forward_text)
    vt = kvt[:, :, 128:256].reshape(512, 128)
    kt_all = kvt[:, :, 0:128].reshape(512, 128)
    oT[...] += dot_tn(vt, ets[8])

    rcp = 1.0 / tot[0:1, :]
    att = (oT[...] * rcp).astype(BF).astype(F32)
    dOTf = dOT[...].astype(F32)
    delta = jnp.sum(dOTf * att, axis=0, keepdims=True)
    tot[0:1, :] = rcp
    tot[1:2, :] = delta
    q2[...] = (qT[...].astype(F32) * rcp).T.astype(BF)
    dO2[...] = (dOTf * rcp).T.astype(BF)
    oT[...] = jnp.zeros_like(oT)

    def back(k, v, eb):
        dp = dot(v, dOT[...])
        ds = (eb.astype(F32) * (dp - tot[1:2, :])).astype(BF)
        oT[...] += dot_tn(k, ds)
        return (dot(ds, q2[...]) * SCALE).astype(BF), dot(eb, dO2[...]).astype(BF)

    def dk_copy(r):
        return remote(dkvs.at[r], dkvr.at[r], dk_ss.at[r], dk_rs.at[r], sdev(r, -1))

    def dt_copy(r):
        return remote(dkvts.at[r], dkvtr.at[r], dt_ss.at[r], dt_rs.at[r], sdev(r, -1))

    def backward(i):
        r = (i + 1) % 8
        gk, gv = back(kv[r, :, 0:128], kv[r, :, 128:256], ets[r])
        dkvs[r, :, 0:128] = gk
        dkvs[r, :, 128:256] = gv

        @pl.when(r != 0)
        def _():
            dk_copy(r).start()

    loop(0, 7, backward)
    gk, gv = back(kt_all, vt, ets[8])
    dkvts[:, :, 0:128] = gk.reshape(8, 64, 128)
    dkvts[:, :, 128:256] = gv.reshape(8, 64, 128)
    loop(1, 8, lambda r: dt_copy(r).start())
    backward(7)

    dq = (oT[...] * (tot[0:1, :] * SCALE)).T
    gq[128:, 0:128] = norm_back(qkvp[128:, 0:128], gains[2:3, :], dq[128:]).astype(BF)
    gq[0:64, 0:128] = norm_back(qkvp[0:64, 0:128], gains[0:1, :], dq[0:64]).astype(BF)

    wsum[0:64, 0:256] = dkvts[0].astype(F32)

    def add_t(r):
        dt_copy(r).wait_recv()
        wsum[0:64, 0:256] += dkvtr[r].astype(F32)

    loop(1, 8, add_t)
    gq[0:64, 128:256] = norm_back(
        qkvp[0:64, 128:256], gains[1:2, :], wsum[0:64, 0:128]).astype(BF)
    gq[0:64, 256:384] = wsum[0:64, 128:256].astype(BF)

    def gf_copy(r):
        return remote(gtf.at[0], gtf.at[r], gf_ss.at[r], gf_rs.at[r], fdev(r, 1))

    def gs_copy(r):
        return remote(gts.at[0], gts.at[r], gs_ss.at[r], gs_rs.at[r], sdev(r, 1))

    gtf[0] = gq[0:64, :]
    gts[0] = gq[0:64, :]
    loop(1, 8, lambda r: gf_copy(r).start())
    loop(1, 8, lambda r: gs_copy(r).start())

    wsum[:, 0:256] = dkvs[0].astype(F32)

    def add_k(r):
        dk_copy(r).wait_recv()
        wsum[:, 0:256] += dkvr[r].astype(F32)

    loop(1, 8, add_k)
    gq[128:, 128:256] = norm_back(
        qkvp[128:, 128:256], gains[3:4, :], wsum[:, 0:128]).astype(BF)
    gq[128:, 256:384] = wsum[:, 128:256].astype(BF)

    other_rows = pl.ds(pl.multiple_of(128 + o * 256, 128), 256)

    def px_copy(r):
        return remote(pxs.at[r], pxr.at[r], ph_ss.at[0, r], ph_rs.at[0, r], pdev)

    def partner_part(r):
        pxs[r] = dot_nt(gq[other_rows, :], W[r]).astype(BF)
        px_copy(r).start()

    loop(0, 8, partner_part)

    def dw_copy(r):
        return remote(dws.at[r], dwr.at[r], dw_ss.at[r], dw_rs.at[r], sdev(r, 1))

    def weight_part(i):
        r = (i + 1) % 8
        dws[r] = dot_tn(hid[chip_at(r, 1)], gq[128:, :]).astype(BF)

        @pl.when(r != 0)
        def _():
            dw_copy(r).start()

    def ph_copy(r):
        return remote(phs.at[r], phr.at[r], ph_ss.at[1, r], ph_rs.at[1, r], fdev(r, -1))

    s1v[...] = jnp.zeros_like(s1v)
    s2v[...] = jnp.zeros_like(s2v)

    def hidden_part(i):
        r = (i + 1) % 8
        b = f_at(r, -1)
        px_copy(r).wait_recv()
        p = (dot_nt(gq[img_rows, :], W[r]) + pxr[r].astype(F32)).astype(BF)
        phs[r] = p

        @pl.when(r != 0)
        def _():
            ph_copy(r).start()

        t = p.astype(F32) * sc[1, b, 0:1, :]
        u = t * nimg[b]
        s1v[...] += t[:, 0:128] + t[:, 128:256] + t[:, 256:384]
        s2v[...] += u[:, 0:128] + u[:, 128:256] + u[:, 256:384]

    def both(i):
        weight_part(i)
        hidden_part(i)

    loop(0, 8, both)

    lane = lax.broadcasted_iota(jnp.int32, (256, 128), 1)
    s1 = jnp.sum(s1v[...], axis=-1, keepdims=True)
    s2 = jnp.sum(s2v[...], axis=-1, keepdims=True)
    sts[...] = jnp.where(lane == 0, s1, s2).T[0:8]

    def st_copy(r):
        return remote(sts, str_.at[r], st_ss.at[r], st_rs.at[r], fdev(r, 1))

    loop(1, 8, lambda r: st_copy(r).start())

    thx[...] = jnp.zeros_like(thx)

    def txt_hidden(r):
        @pl.when(r != 0)
        def _():
            gf_copy(r).wait_recv()

        thx[...] += dot_nt(gtf[r], wt[(r // 4) * 4 + (4 - r % 4) % 4])

    loop(0, 8, txt_hidden)
    their = pl.ds(pl.multiple_of(o * 32, 32), 32)
    cp_th = remote(thx.at[their], thr, p_ss.at[4], p_rs.at[4], pdev)
    cp_th.start()

    loop(1, 8, lambda r: gs_copy(r).wait_recv())
    loop(1, 8, lambda r: h_copy(r).wait_recv())
    wxt[...] = dot_tn(htg[...].reshape(512, 384), gts[...].reshape(512, 384))
    mine = pl.ds(pl.multiple_of(c * 192, 64), 192)
    theirs = pl.ds(pl.multiple_of(o * 192, 64), 192)
    cp_wt = remote(wxt.at[theirs], wxtr, p_ss.at[5], p_rs.at[5], pdev)
    cp_wt.start()

    cp_th.wait_recv()
    gh = thx[txt_rows, :] + thr[...]
    tsc = gh * sc[0, f, 0:1, :]
    tn = ntxt[f]
    t1 = jnp.sum(tsc, axis=-1, keepdims=True)
    t2 = jnp.sum(tsc * tn, axis=-1, keepdims=True)
    lane_t = lax.broadcasted_iota(jnp.int32, (32, 128), 1)
    tsts[...] = jnp.where(lane_t == 0, t1, t2)

    def ts_copy(r):
        return remote(tsts, tstr.at[r], ts_ss.at[r], ts_rs.at[r], fdev(r, 1))

    loop(1, 8, lambda r: ts_copy(r).start())
    thr[...] = tsc

    def place(out, part, head):
        for j in range(3):
            out[j, :, pl.ds(m128(head * 128), 128)] = part[:, j * 128:(j + 1) * 128]

    cp_wt.wait_recv()
    place(dw_txt, wxt[mine, :], c)
    place(dw_txt, wxtr[...], o)

    st = sts[...]
    for r in range(1, 8):
        st_copy(r).wait_recv()
        st = st + str_[r]
    stT = jnp.concatenate([st, jnp.zeros((120, 256), F32)], axis=0).T
    acc = phs[0].astype(F32)
    for r in range(1, 8):
        ph_copy(r).wait_recv()
        acc = acc + phr[r].astype(F32)
    scaled = acc * sc[1, f, 0:1, :]
    dx_img[...] = (invi[:, 0:1] * (
        scaled - stT[:, 0:1] * (1.0 / 3072) - nimg[f] * (stT[:, 1:2] * (1.0 / 3072))
    )).astype(BF)

    tt = tsts[...]
    for r in range(1, 8):
        ts_copy(r).wait_recv()
        tt = tt + tstr[r]
    dx_txt[...] = (invt[:, 0:1] * (
        thr[...] - tt[:, 0:1] * (1.0 / 3072) - ntxt[f] * (tt[:, 1:2] * (1.0 / 3072))
    )).astype(BF)

    wx[...] = dws[0].astype(F32)

    def add_w(r):
        dw_copy(r).wait_recv()
        wx[...] += dwr[r].astype(F32)

    loop(1, 8, add_w)
    cp_wi = remote(wx.at[theirs], wxr, p_ss.at[6], p_rs.at[6], pdev)
    cp_wi.start()
    place(dw_img, wx[mine, :], c)
    cp_wi.wait_recv()
    place(dw_img, wxr[...], o)

    def drain(r):
        for j in range(3):
            w_copy(r, j).wait_send()
        for cp in (t_copy, h_copy, kv_copy, kt_copy, dk_copy, dt_copy, gf_copy, gs_copy,
                   dw_copy, ph_copy, st_copy, ts_copy):
            cp(r).wait_send()

    loop(1, 8, drain)
    loop(0, 8, lambda r: px_copy(r).wait_send())
    for cp in (cp_coti, cp_cott, cp_ht, cp_hi, cp_th, cp_wt, cp_wi):
        cp.wait_send()


def scratch():
    V = pltpu.VMEM
    return [
        V((256, 3072), BF), V((32, 3072), BF), V((2, 256, 6144), BF), V((2, 8, 6144), F32),
        V((2, 8, 8, 384), F32), V((8, 384, 384), BF), V((8, 384, 384), BF),
        V((8, 512, 384), BF), V((8, 64, 384), BF), V((8, 64, 384), BF),
        V((8, 256, 384), F32), V((8, 32, 384), F32), V((256, 128), F32), V((32, 128), F32),
        V((8, 64, 384), BF), V((8, 64, 384), BF), V((640, 384), F32), V((640, 128), BF),
        V((128, 640), BF), V((128, 640), BF), V((640, 128), BF), V((640, 128), BF),
        V((8, 512, 256), BF), V((8, 64, 256), BF), V((9, 512, 640), BF),
        V((8, 512, 256), BF), V((8, 512, 256), BF), V((8, 64, 256), BF), V((8, 64, 256), BF),
        V((128, 640), F32), V((8, 640), F32), V((640, 384), BF),
        V((8, 64, 384), BF), V((8, 64, 384), BF), V((8, 384, 384), BF), V((8, 384, 384), BF),
        V((8, 256, 384), BF), V((8, 256, 384), BF), V((8, 256, 384), BF), V((8, 256, 384), BF),
        V((256, 128), F32), V((256, 128), F32), V((8, 256), F32), V((8, 8, 256), F32),
        V((64, 384), F32), V((32, 384), F32), V((32, 128), F32), V((8, 32, 128), F32),
        V((384, 384), F32), V((192, 384), F32), V((384, 384), F32), V((192, 384), F32),
        V((512, 256), F32),
    ] + [
        pltpu.SemaphoreType.DMA(shape)
        for shape in (
            [(6,), (3,), (8, 3), (8, 3), (8, 3), (7,), (7,)] + [(8,)] * 18 + [(2, 8)] * 2
            + [(8,)] * 4
        )
    ]


def on_device(
    img_tokens, txt_tokens, img_weight, txt_weight, img_modulation, txt_modulation, qk_gains,
    timestep, valid_text, img_cotangent, txt_cotangent,
):
    features = time_features(timestep, img_modulation.shape[0])
    feat = jnp.broadcast_to(features, (16, features.shape[1]))
    gains = jnp.concatenate([qk_gains.reshape(4, HD), jnp.zeros((4, HD), F32)], 0)
    live = jnp.broadcast_to(
        (jnp.arange(512, dtype=jnp.int32) < valid_text[0]).astype(F32)[:, None], (512, 128))
    anys = pl.BlockSpec(memory_space=pl.ANY)
    vm = pl.BlockSpec(memory_space=pltpu.VMEM)
    dw_img, dw_txt, dx_img, dx_txt = pl.pallas_call(
        kernel,
        out_shape=(
            jax.ShapeDtypeStruct((3, 192, 256), F32),
            jax.ShapeDtypeStruct((3, 192, 256), F32),
            jax.ShapeDtypeStruct((256, 384), BF),
            jax.ShapeDtypeStruct((32, 384), BF),
        ),
        in_specs=[anys] * 6 + [vm] * 3 + [anys] * 2,
        out_specs=[vm] * 4,
        scratch_shapes=scratch(),
        compiler_params=pltpu.CompilerParams(
            collective_id=0, has_side_effects=True, vmem_limit_bytes=62 * 2 ** 20),
        name="joint_block",
    )(
        img_tokens, txt_tokens, jnp.transpose(img_weight, (1, 0, 2)),
        jnp.transpose(txt_weight, (1, 0, 2)), img_modulation, txt_modulation, feat, gains, live,
        img_cotangent, txt_cotangent,
    )
    return (
        jnp.transpose(dw_img, (1, 0, 2)), jnp.transpose(dw_txt, (1, 0, 2)), dx_img, dx_txt
    )


def solution(mesh):
    return jax.shard_map(
        on_device,
        mesh=mesh,
        in_specs=(
            P("seq", None),
            P("seq", None),
            P("fsdp", None, None),
            P("fsdp", None, None),
            P(),
            P(),
            P(),
            P(),
            P(),
            P("seq", "fsdp"),
            P("seq", "fsdp"),
        ),
        out_specs=(
            P("seq", None, "fsdp"),
            P("seq", None, "fsdp"),
            P("seq", "fsdp"),
            P("seq", "fsdp"),
        ),
        check_vma=False,
    )
```

time: 550 us -> 177 us (0.32)
  waiting for transfers between devices: 386 us -> 0 us
  Pallas kernels: 0 us -> 165 us
  local copies, waits for them, and re-layouts: 61.6 us -> 9.52 us
  matrix products: 43.3 us -> 0 us
  other arithmetic: 26.6 us -> 0.07 us
  between operations: 15.7 us -> 1.95 us
  starting transfers between devices: 12.7 us -> 0 us
    pallas_call x0 -> x1, Pallas kernels: none -> 165 us  [on_device(): pl.pallas_call(kernel, out_shape=(jax.ShapeDtypeStruct((3, 192, 256), F32...]
    reduce_scatter x2 -> x0, waiting for transfers between devices: 133 us -> none  [the longest x1 74.1 us: on_device(): lax.psum_scatter(weight_terms().astype(jnp.bfloat16), 'seq', scatter_dime...]
    all_to_all x2 -> x0, waiting for transfers between devices: 116 us -> none  [the longest x1 62.2 us: on_device(): lax.all_to_all(txt_weight, 'fsdp', split_axis=2, concat_axis=0, tiled=True)]
    psum x1 -> x0, waiting for transfers between devices: 79.3 us -> none  [on_device(): lax.psum(hidden_part.astype(jnp.bfloat16), 'fsdp').astype(jnp.float32)]
    all_gather x2 -> x0, waiting for transfers between devices: 58.6 us -> none  [the longest x1 34 us: on_device(): lax.all_gather(keys_own, 'seq', axis=0, tiled=True)]
    dot_general x14 -> x0, matrix products: 43.3 us -> none  [the longest x2 7.76 us: weight_terms(): jnp.einsum('nc,nw->cw', streams[which][0], grad_flat[which], preferred_el...]
    unnamed x50 -> x4, local copies, waits for them, and re-layouts: 36.9 us -> 6.8 us
    all_to_all x2 -> x0, local copies, waits for them, and re-layouts: 12.8 us -> none  [the longest x1 6.39 us: on_device(): lax.all_to_all(txt_weight, 'fsdp', split_axis=2, concat_axis=0, tiled=True)]
  transfers between devices with their start and end apart: 7 -> 0, of which waited for: 7 -> 0; matrix products, arithmetic and copies ran while one was open for 11% -> 0% of each run, Pallas kernels for 0% -> 0%
where the time goes in v1:
time: 177 us
  Pallas kernels  165 us (93%)
  local copies, waits for them, and re-layouts  9.52 us (5%)
  between operations  1.95 us (1%)
    pallas_call x1, Pallas kernels, on_device(): pl.pallas_call(kernel, out_shape=(jax.ShapeDtypeStruct((3, 192, 256), F32...  165 us
    unnamed x4, local copies, waits for them, and re-layouts  6.8 us

profile of v1, /device:TPU:1, one launch (start us, length us, event | category | flops | bytes accessed | tf_op | source)
XLA Modules:
  0.0 176.9 jit_solution(10336370151320965089)
XLA Ops:
  2.0 1.3 concatenate.17.gains
  3.3 0.6 broadcast_in_dim.4.feat
  3.9 0.8 broadcast_in_dim.5.live
  4.7 165.3 %joint_block.1 = (f32[3,192,256]{2,1,0:T(8,128)}, f32[3,192,256]{2,1,0:T(8,128)}, bf16[256,384]{1,0:T(8,128)(2,1)}, bf16[32,384]{1,0:T(8,128)(2,1)}) custom-call(bf16[256,3072]{1,0:T(8,128)(2,1)} %x_img.1, bf16[32,3072]{1,0:T(8,128)(2,1)} %x_txt.1, bf16[3,384,2048]{2,1,0:T(8,128)(2,1)} %bitcast.8, bf16[3,384,2048]{2,1,0:T(8,128)(2,1)} %bitcast.9, ...), custom_call_target="tpu_custom_call" | custom-call | tf_op jit(solution)/shard_map/joint_block/pallas_call | solution.py:567
  170.1 1.9 %copy.21 = f32[192,3,256]{2,0,1:T(8,128)} copy(f32[192,3,256]{2,0,1:T(8,128)} %bitcast.11) | data formatting | bytes 1179648
  172.0 1.9 %copy.22 = f32[192,3,256]{2,0,1:T(8,128)} copy(f32[192,3,256]{2,0,1:T(8,128)} %bitcast.10) | data formatting | bytes 1179648
  173.9 1.6 copy.23
  175.5 1.3 copy.24
  (3 shorter events, 0.1 us)

commit v2 on v1

--- a/solution.py
+++ b/solution.py
@@ -44,15 +44,15 @@
 
 
 def kernel(
-    x_img, x_txt, w_img, w_txt, mod_img, mod_txt, feat, gains, live, cot_img, cot_txt,
+    x_img, x_txt, w_img, w_txt, mod_img, mod_txt, feat, gains, valid, cot_img, cot_txt,
     dw_img, dw_txt, dx_img, dx_txt,
     xi, xt, mods, mixed, sc, W, wt, hid, hidt, htg, nimg, ntxt, invi, invt,
-    tps, tpr, qkvp, dO, qT, dOT, q2, dO2, kv, kvt, ets, dkvs, dkvr, dkvts, dkvtr,
-    oT, tot, gq, gtf, gts, dws, dwr, pxs, pxr, phs, phr, s1v, s2v, sts, str_,
-    thx, thr, tsts, tstr, wx, wxr, wxt, wxtr, wsum,
-    lsem, wl_sem, wtl_sem, w_ss, w_rs, p_ss, p_rs, t_ss, t_rs, h_ss, h_rs,
+    tps, tpr, qkvp, dO, qr, qT, dOT, q2, dO2, kv, kvt, ets, etx, dkvs, dkvr, dkvts, dkvtr,
+    oT, stx, stxr, dqf, dqr, gq, gtf, gts, dws, dwr, pxs, pxr, phs, phr, s1v, s2v, sts, str_,
+    thx, thr, tsts, tstr, wx, wxr, wxt, wxtr, wsum, wcs, wcr,
+    lsem, wl_sem, wtl_sem, w_ss, w_rs, p_ss, p_rs, x_ss, x_rs, t_ss, t_rs, h_ss, h_rs,
     kv_ss, kv_rs, kt_ss, kt_rs, dk_ss, dk_rs, dt_ss, dt_rs, gf_ss, gf_rs, gs_ss, gs_rs,
-    dw_ss, dw_rs, ph_ss, ph_rs, st_ss, st_rs, ts_ss, ts_rs,
+    dq_ss, dq_rs, dw_ss, dw_rs, ph_ss, ph_rs, st_ss, st_rs, ts_ss, ts_rs,
 ):
     s = lax.axis_index("seq")
     f = lax.axis_index("fsdp")
@@ -74,6 +74,8 @@
         return (chip_at(r, sign) * 2 + c, f)
 
     pdev = (chip * 2 + o, f)
+    xdev = sdev(4, 1)
+    xo = 1 - xlo
 
     def remote(src, dst, ss, rs, dev):
         return pltpu.make_async_remote_copy(
@@ -97,10 +99,10 @@
         pltpu.make_async_copy(mod_txt, mods.at[0], lsem.at[3]),
         pltpu.make_async_copy(
             cot_img.at[:, pl.ds(m128(c * 128), 128)],
-            dO.at[pl.ds(pl.multiple_of(128 + c * 256, 128), 256)], lsem.at[4]),
+            dO.at[pl.ds(pl.multiple_of(128 + xlo * 512 + c * 256, 128), 256)], lsem.at[4]),
         pltpu.make_async_copy(
             cot_txt.at[:, pl.ds(m128(c * 128), 128)],
-            dO.at[pl.ds(pl.multiple_of(c * 32, 32), 32)], lsem.at[5]),
+            dO.at[pl.ds(pl.multiple_of(xlo * 64 + c * 32, 32), 32)], lsem.at[5]),
     ]
     for cp in loc:
         cp.start()
@@ -150,16 +152,19 @@
     img_rows = pl.ds(pl.multiple_of(128 + c * 256, 128), 256)
     txt_rows = pl.ds(pl.multiple_of(c * 32, 32), 32)
     half_rows = pl.ds(pl.multiple_of(c * 256, 256), 256)
-    cp_coti = remote(cot_img.at[:, pl.ds(m128(o * 128), 128)], dO.at[img_rows],
+    cp_coti = remote(cot_img.at[:, pl.ds(m128(o * 128), 128)],
+                     dO.at[pl.ds(pl.multiple_of(128 + xlo * 512 + c * 256, 128), 256)],
                      p_ss.at[0], p_rs.at[0], pdev)
-    cp_cott = remote(cot_txt.at[:, pl.ds(m128(o * 128), 128)], dO.at[txt_rows],
+    cp_cott = remote(cot_txt.at[:, pl.ds(m128(o * 128), 128)],
+                     dO.at[pl.ds(pl.multiple_of(xlo * 64 + c * 32, 32), 32)],
                      p_ss.at[1], p_rs.at[1], pdev)
     cp_coti.start()
     cp_cott.start()
 
     for which in (0, 1):
         loc[3 - which].wait()
-        mixed[which] = dot(feat[...], mods[which])[:8]
+        row = jnp.broadcast_to(feat[...].astype(F32), (16, 256)).astype(BF)
+        mixed[which] = dot(row, mods[which])[:8]
         for b in range(8):
             sc[which, b] = 1.0 + mixed[which, :, 3072 + b * 384:3072 + (b + 1) * 384]
 
@@ -217,12 +222,16 @@
     htg[0] = hidt[chip]
     loop(1, 8, lambda r: h_copy(r).start())
 
+    own_t = pl.ds(pl.multiple_of(xlo * 64, 64), 64)
+    own_i = pl.ds(pl.multiple_of(128 + xlo * 512, 128), 512)
     loc[4].wait()
     loc[5].wait()
     cp_coti.wait_recv()
     cp_cott.wait_recv()
-    dO[64:128, :] = jnp.zeros((64, 128), BF)
-    dOT[...] = dO[...].astype(F32).T.astype(BF)
+    cp_xot = remote(dO.at[own_t], dO.at[own_t], x_ss.at[0], x_rs.at[0], xdev)
+    cp_xoi = remote(dO.at[own_i], dO.at[own_i], x_ss.at[1], x_rs.at[1], xdev)
+    cp_xot.start()
+    cp_xoi.start()
 
     cp_hi.wait_recv()
     for j in range(3):
@@ -245,16 +254,10 @@
 
     loop(1, 8, txt_add)
 
-    def normed_heads(lo, hi, g0):
-        a = qkvp[lo:hi, 0:128]
-        b = qkvp[lo:hi, 128:256]
-        qn = a * lax.rsqrt(jnp.mean(a * a, axis=-1, keepdims=True) + EPS) * gains[g0:g0 + 1, :]
-        kn = b * lax.rsqrt(jnp.mean(b * b, axis=-1, keepdims=True) + EPS) * gains[g0 + 1:g0 + 2, :]
-        qT[:, lo:hi] = qn.T.astype(BF)
-        return kn.astype(BF)
-
-    kv[0, :, 0:128] = normed_heads(128, 640, 2)
-    kv[0, :, 128:256] = qkvp[128:, 256:384].astype(BF)
+    def normed_head(lo, hi, col, g):
+        a = qkvp[lo:hi, col:col + 128]
+        return (a * lax.rsqrt(jnp.mean(a * a, axis=-1, keepdims=True) + EPS)
+                * gains[g:g + 1, :]).astype(BF)
 
     def kv_copy(r):
         return remote(kv.at[0], kv.at[r], kv_ss.at[r], kv_rs.at[r], sdev(r, 1))
@@ -262,54 +265,74 @@
     def kt_copy(r):
         return remote(kvt.at[0], kvt.at[r], kt_ss.at[r], kt_rs.at[r], sdev(r, 1))
 
-    loop(1, 8, lambda r: kv_copy(r).start())
-    kt = normed_heads(0, 128, 0)
-    kvt[0, :, 0:128] = kt[0:64]
+    kv[0, :, 0:128] = normed_head(128, 640, 128, 3)
+    kv[0, :, 128:256] = qkvp[128:, 256:384].astype(BF)
+    loop(1, 4, lambda r: kv_copy(r).start())
+    kvt[0, :, 0:128] = normed_head(0, 64, 128, 1)
     kvt[0, :, 128:256] = qkvp[0:64, 256:384].astype(BF)
-    loop(1, 8, lambda r: kt_copy(r).start())
+    loop(1, 4, lambda r: kt_copy(r).start())
+    qr[own_i, :] = normed_head(128, 640, 0, 2)
+    qr[own_t, :] = normed_head(0, 64, 0, 0)
+    cp_xqt = remote(qr.at[own_t], qr.at[own_t], x_ss.at[2], x_rs.at[2], xdev)
+    cp_xqi = remote(qr.at[own_i], qr.at[own_i], x_ss.at[3], x_rs.at[3], xdev)
+    cp_xqi.start()
+    cp_xqt.start()
+    cp_xot.wait_recv()
+    cp_xoi.wait_recv()
+    dOT[...] = dO[...].astype(F32).T.astype(BF)
+    cp_xqi.wait_recv()
+    cp_xqt.wait_recv()
+    qT[...] = qr[...].astype(F32).T.astype(BF)
 
     oT[...] = jnp.zeros_like(oT)
-    tot[...] = jnp.zeros_like(tot)
-
-    def forward(r):
-        @pl.when(r != 0)
+    stx[...] = jnp.zeros_like(stx)
+
+    def half_of(i):
+        return pl.ds(pl.multiple_of((i % 2) * 256, 256), 256)
+
+    def forward(i):
+        r = i // 2
+
+        @pl.when((i % 2 == 0) & (r != 0))
         def _():
             kv_copy(r).wait_recv()
 
-        e = jnp.exp2(dot(kv[r, :, 0:128], qT[...]) * EXP2)
-        tot[0:1, :] += jnp.sum(e, axis=0, keepdims=True)
+        e = jnp.exp2(dot(kv[r, half_of(i), 0:128], qT[...]) * EXP2)
+        stx[0:1, :] += jnp.sum(e, axis=0, keepdims=True)
         eb = e.astype(BF)
-        ets[r] = eb
-        oT[...] += dot_tn(kv[r, :, 128:256], eb)
+        ets[i] = eb
+        oT[...] += dot_tn(kv[r, half_of(i), 128:256], eb)
 
     loop(0, 8, forward)
-    loop(1, 8, lambda r: kt_copy(r).wait_recv())
+    loop(1, 4, lambda r: kt_copy(r).wait_recv())
 
     def forward_text(r):
-        rows = pl.ds(pl.multiple_of(r * 64, 64), 64)
         e = jnp.exp2(dot(kvt[r, :, 0:128], qT[...]) * EXP2)
-        e = e * live[pl.ds(pl.multiple_of(chip_at(r, -1) * 64, 64), 64), 0:1]
-        tot[0:1, :] += jnp.sum(e, axis=0, keepdims=True)
-        ets[8, rows, :] = e.astype(BF)
-
-    loop(0, 8, forward_text)
-    vt = kvt[:, :, 128:256].reshape(512, 128)
-    kt_all = kvt[:, :, 0:128].reshape(512, 128)
-    oT[...] += dot_tn(vt, ets[8])
-
-    rcp = 1.0 / tot[0:1, :]
-    att = (oT[...] * rcp).astype(BF).astype(F32)
-    dOTf = dOT[...].astype(F32)
-    delta = jnp.sum(dOTf * att, axis=0, keepdims=True)
-    tot[0:1, :] = rcp
-    tot[1:2, :] = delta
+        index = chip_at(r, -1) * 64 + lax.broadcasted_iota(jnp.int32, (64, 1152), 0)
+        e = jnp.where(index < valid[0], e, 0.0)
+        stx[0:1, :] += jnp.sum(e, axis=0, keepdims=True)
+        etx[pl.ds(pl.multiple_of(r * 64, 64), 64), :] = e.astype(BF)
+
+    loop(0, 4, forward_text)
+    vt = kvt[:, :, 128:256].reshape(256, 128)
+    kt_all = kvt[:, :, 0:128].reshape(256, 128)
+    oT[...] += dot_tn(vt, etx[...])
+
+    stx[1:2, :] = jnp.sum(dOT[...].astype(F32) * oT[...], axis=0, keepdims=True)
+    cp_st = remote(stx, stxr, x_ss.at[4], x_rs.at[4], xdev)
+    cp_st.start()
+    oT[...] = jnp.zeros_like(oT)
+    cp_st.wait_recv()
+    rcp = 1.0 / (stx[0:1, :] + stxr[0:1, :])
+    delta = (stx[1:2, :] + stxr[1:2, :]) * rcp
+    stxr[2:3, :] = rcp
+    stxr[3:4, :] = delta
     q2[...] = (qT[...].astype(F32) * rcp).T.astype(BF)
-    dO2[...] = (dOTf * rcp).T.astype(BF)
-    oT[...] = jnp.zeros_like(oT)
+    dO2[...] = (dOT[...].astype(F32) * rcp).T.astype(BF)
 
     def back(k, v, eb):
         dp = dot(v, dOT[...])
-        ds = (eb.astype(F32) * (dp - tot[1:2, :])).astype(BF)
+        ds = (eb.astype(F32) * (dp - stxr[3:4, :])).astype(BF)
         oT[...] += dot_tn(k, ds)
         return (dot(ds, q2[...]) * SCALE).astype(BF), dot(eb, dO2[...]).astype(BF)
 
@@ -320,25 +343,57 @@
         return remote(dkvts.at[r], dkvtr.at[r], dt_ss.at[r], dt_rs.at[r], sdev(r, -1))
 
     def backward(i):
-        r = (i + 1) % 8
-        gk, gv = back(kv[r, :, 0:128], kv[r, :, 128:256], ets[r])
-        dkvs[r, :, 0:128] = gk
-        dkvs[r, :, 128:256] = gv
-
-        @pl.when(r != 0)
+        r = (i // 2 + 1) % 4
+        rows = half_of(i)
+        gk, gv = back(kv[r, rows, 0:128], kv[r, rows, 128:256], ets[r * 2 + i % 2])
+        dkvs[r, rows, 0:128] = gk
+        dkvs[r, rows, 128:256] = gv
+
+        @pl.when((i % 2 == 1) & (r != 0))
         def _():
             dk_copy(r).start()
 
-    loop(0, 7, backward)
-    gk, gv = back(kt_all, vt, ets[8])
-    dkvts[:, :, 0:128] = gk.reshape(8, 64, 128)
-    dkvts[:, :, 128:256] = gv.reshape(8, 64, 128)
-    loop(1, 8, lambda r: dt_copy(r).start())
-    backward(7)
-
-    dq = (oT[...] * (tot[0:1, :] * SCALE)).T
-    gq[128:, 0:128] = norm_back(qkvp[128:, 0:128], gains[2:3, :], dq[128:]).astype(BF)
-    gq[0:64, 0:128] = norm_back(qkvp[0:64, 0:128], gains[0:1, :], dq[0:64]).astype(BF)
+    loop(0, 6, backward)
+    gk, gv = back(kt_all, vt, etx[...])
+    dkvts[:, :, 0:128] = gk.reshape(4, 64, 128)
+    dkvts[:, :, 128:256] = gv.reshape(4, 64, 128)
+    loop(1, 4, lambda r: dt_copy(r).start())
+    loop(6, 8, backward)
+
+    dq = (oT[...] * (stxr[2:3, :] * SCALE)).T
+    dO2[...] = dq.astype(BF)
+    qkvp[64:128, 0:128] = dq[0:64]
+    qkvp[64:128, 128:256] = dq[64:128]
+    dqf[0:512, :] = dq[128:640]
+    dqf[512:1024, :] = dq[640:1152]
+    their_t = pl.ds(pl.multiple_of(xo * 64, 64), 64)
+    their_i = pl.ds(pl.multiple_of(128 + xo * 512, 128), 512)
+    cp_dqi = remote(dO2.at[their_i], dqr.at[pl.ds(64, 512)], x_ss.at[5], x_rs.at[5], xdev)
+    cp_dqt = remote(dO2.at[their_t], dqr.at[pl.ds(0, 64)], x_ss.at[6], x_rs.at[6], xdev)
+    cp_dqi.start()
+    cp_dqt.start()
+    cp_dqi.wait_recv()
+    dqi = dqf[pl.ds(pl.multiple_of(xlo * 512, 512), 512), :] + dqr[64:576, :].astype(F32)
+    gq[128:, 0:128] = norm_back(qkvp[128:, 0:128], gains[2:3, :], dqi).astype(BF)
+
+    def dw_copy(r, part):
+        cols = pl.ds(0, 128) if part == 0 else pl.ds(128, 256)
+        ss, rs = (dq_ss, dq_rs) if part == 0 else (dw_ss, dw_rs)
+        return remote(dws.at[r, :, cols], dwr.at[r, :, cols], ss.at[r], rs.at[r], sdev(r % 4, 1))
+
+    def weight_part(i, part):
+        r = ((i // 4 + 1) % 2) * 4 + (i + 1) % 4
+        lo, hi = (0, 128) if part == 0 else (128, 384)
+        dws[r, :, lo:hi] = dot_tn(hid[chip_at(r, 1)], gq[128:, lo:hi]).astype(BF)
+
+        @pl.when(r % 4 != 0)
+        def _():
+            dw_copy(r, part).start()
+
+    loop(0, 8, lambda i: weight_part(i, 0))
+    cp_dqt.wait_recv()
+    dqt = jnp.where(xlo == 0, qkvp[64:128, 0:128], qkvp[64:128, 128:256]) + dqr[0:64, :].astype(F32)
+    gq[0:64, 0:128] = norm_back(qkvp[0:64, 0:128], gains[0:1, :], dqt).astype(BF)
 
     wsum[0:64, 0:256] = dkvts[0].astype(F32)
 
@@ -346,7 +401,7 @@
         dt_copy(r).wait_recv()
         wsum[0:64, 0:256] += dkvtr[r].astype(F32)
 
-    loop(1, 8, add_t)
+    loop(1, 4, add_t)
     gq[0:64, 128:256] = norm_back(
         qkvp[0:64, 128:256], gains[1:2, :], wsum[0:64, 0:128]).astype(BF)
     gq[0:64, 256:384] = wsum[0:64, 128:256].astype(BF)
@@ -368,7 +423,7 @@
         dk_copy(r).wait_recv()
         wsum[:, 0:256] += dkvr[r].astype(F32)
 
-    loop(1, 8, add_k)
+    loop(1, 4, add_k)
     gq[128:, 128:256] = norm_back(
         qkvp[128:, 128:256], gains[3:4, :], wsum[:, 0:128]).astype(BF)
     gq[128:, 256:384] = wsum[:, 128:256].astype(BF)
@@ -383,17 +438,6 @@
         px_copy(r).start()
 
     loop(0, 8, partner_part)
-
-    def dw_copy(r):
-        return remote(dws.at[r], dwr.at[r], dw_ss.at[r], dw_rs.at[r], sdev(r, 1))
-
-    def weight_part(i):
-        r = (i + 1) % 8
-        dws[r] = dot_tn(hid[chip_at(r, 1)], gq[128:, :]).astype(BF)
-
-        @pl.when(r != 0)
-        def _():
-            dw_copy(r).start()
 
     def ph_copy(r):
         return remote(phs.at[r], phr.at[r], ph_ss.at[1, r], ph_rs.at[1, r], fdev(r, -1))
@@ -418,7 +462,7 @@
         s2v[...] += u[:, 0:128] + u[:, 128:256] + u[:, 256:384]
 
     def both(i):
-        weight_part(i)
+        weight_part(i, 1)
         hidden_part(i)
 
     loop(0, 8, both)
@@ -500,13 +544,20 @@
         thr[...] - tt[:, 0:1] * (1.0 / 3072) - ntxt[f] * (tt[:, 1:2] * (1.0 / 3072))
     )).astype(BF)
 
+    def add_w(r):
+        dw_copy(r, 0).wait_recv()
+        dw_copy(r, 1).wait_recv()
+        wx[...] += dwr[r].astype(F32)
+
+    wx[...] = dws[4].astype(F32)
+    loop(5, 8, add_w)
+    wcs[...] = wx[...].astype(BF)
+    cp_wc = remote(wcs, wcr, x_ss.at[7], x_rs.at[7], xdev)
+    cp_wc.start()
     wx[...] = dws[0].astype(F32)
-
-    def add_w(r):
-        dw_copy(r).wait_recv()
-        wx[...] += dwr[r].astype(F32)
-
-    loop(1, 8, add_w)
+    loop(1, 4, add_w)
+    cp_wc.wait_recv()
+    wx[...] += wcr[...].astype(F32)
     cp_wi = remote(wx.at[theirs], wxr, p_ss.at[6], p_rs.at[6], pdev)
     cp_wi.start()
     place(dw_img, wx[mine, :], c)
@@ -516,14 +567,31 @@
     def drain(r):
         for j in range(3):
             w_copy(r, j).wait_send()
-        for cp in (t_copy, h_copy, kv_copy, kt_copy, dk_copy, dt_copy, gf_copy, gs_copy,
-                   dw_copy, ph_copy, st_copy, ts_copy):
+        for cp in (t_copy, h_copy, gf_copy, gs_copy, ph_copy, st_copy, ts_copy):
             cp(r).wait_send()
 
+        @pl.when(r % 4 != 0)
+        def _():
+            dw_copy(r, 0).wait_send()
+            dw_copy(r, 1).wait_send()
+
+    def drain_z(r):
+        for cp in (kv_copy, kt_copy, dk_copy, dt_copy):
+            cp(r).wait_send()
+
     loop(1, 8, drain)
+    loop(1, 4, drain_z)
     loop(0, 8, lambda r: px_copy(r).wait_send())
-    for cp in (cp_coti, cp_cott, cp_ht, cp_hi, cp_th, cp_wt, cp_wi):
+    for cp in (cp_coti, cp_cott, cp_ht, cp_hi, cp_th, cp_wt, cp_wi, cp_xot, cp_xoi, cp_xqt,
+               cp_xqi, cp_st, cp_dqi, cp_dqt, cp_wc):
         cp.wait_send()
+
+
+def finish(a, b, c, d, oa, ob, oc, od):
+    oa[...] = a[...]
+    ob[...] = b[...]
+    oc[...] = c[...]
+    od[...] = d[...]
 
 
 def scratch():
@@ -533,22 +601,24 @@
         V((2, 8, 8, 384), F32), V((8, 384, 384), BF), V((8, 384, 384), BF),
         V((8, 512, 384), BF), V((8, 64, 384), BF), V((8, 64, 384), BF),
         V((8, 256, 384), F32), V((8, 32, 384), F32), V((256, 128), F32), V((32, 128), F32),
-        V((8, 64, 384), BF), V((8, 64, 384), BF), V((640, 384), F32), V((640, 128), BF),
-        V((128, 640), BF), V((128, 640), BF), V((640, 128), BF), V((640, 128), BF),
-        V((8, 512, 256), BF), V((8, 64, 256), BF), V((9, 512, 640), BF),
-        V((8, 512, 256), BF), V((8, 512, 256), BF), V((8, 64, 256), BF), V((8, 64, 256), BF),
-        V((128, 640), F32), V((8, 640), F32), V((640, 384), BF),
+        V((8, 64, 384), BF), V((8, 64, 384), BF), V((640, 384), F32), V((1152, 128), BF),
+        V((1152, 128), BF), V((128, 1152), BF), V((128, 1152), BF), V((1152, 128), BF),
+        V((1152, 128), BF),
+        V((4, 512, 256), BF), V((4, 64, 256), BF), V((8, 256, 1152), BF), V((256, 1152), BF),
+        V((4, 512, 256), BF), V((4, 512, 256), BF), V((4, 64, 256), BF), V((4, 64, 256), BF),
+        V((128, 1152), F32), V((8, 1152), F32), V((8, 1152), F32), V((1024, 128), F32),
+        V((576, 128), BF), V((640, 384), BF),
         V((8, 64, 384), BF), V((8, 64, 384), BF), V((8, 384, 384), BF), V((8, 384, 384), BF),
         V((8, 256, 384), BF), V((8, 256, 384), BF), V((8, 256, 384), BF), V((8, 256, 384), BF),
         V((256, 128), F32), V((256, 128), F32), V((8, 256), F32), V((8, 8, 256), F32),
         V((64, 384), F32), V((32, 384), F32), V((32, 128), F32), V((8, 32, 128), F32),
         V((384, 384), F32), V((192, 384), F32), V((384, 384), F32), V((192, 384), F32),
-        V((512, 256), F32),
+        V((512, 256), F32), V((384, 384), BF), V((384, 384), BF),
     ] + [
         pltpu.SemaphoreType.DMA(shape)
         for shape in (
-            [(6,), (3,), (8, 3), (8, 3), (8, 3), (7,), (7,)] + [(8,)] * 18 + [(2, 8)] * 2
-            + [(8,)] * 4
+            [(6,), (3,), (8, 3), (8, 3), (8, 3), (7,), (7,), (8,), (8,)] + [(8,)] * 4
+            + [(4,)] * 8 + [(8,)] * 8 + [(2, 8)] * 2 + [(8,)] * 4
         )
     ]
 
@@ -558,10 +628,6 @@
     timestep, valid_text, img_cotangent, txt_cotangent,
 ):
     features = time_features(timestep, img_modulation.shape[0])
-    feat = jnp.broadcast_to(features, (16, features.shape[1]))
-    gains = jnp.concatenate([qk_gains.reshape(4, HD), jnp.zeros((4, HD), F32)], 0)
-    live = jnp.broadcast_to(
-        (jnp.arange(512, dtype=jnp.int32) < valid_text[0]).astype(F32)[:, None], (512, 128))
     anys = pl.BlockSpec(memory_space=pl.ANY)
     vm = pl.BlockSpec(memory_space=pltpu.VMEM)
     dw_img, dw_txt, dx_img, dx_txt = pl.pallas_call(
@@ -572,7 +638,7 @@
             jax.ShapeDtypeStruct((256, 384), BF),
             jax.ShapeDtypeStruct((32, 384), BF),
         ),
-        in_specs=[anys] * 6 + [vm] * 3 + [anys] * 2,
+        in_specs=[anys] * 6 + [vm] * 2 + [pl.BlockSpec(memory_space=pltpu.SMEM)] + [anys] * 2,
         out_specs=[vm] * 4,
         scratch_shapes=scratch(),
         compiler_params=pltpu.CompilerParams(
@@ -580,9 +646,13 @@
         name="joint_block",
     )(
         img_tokens, txt_tokens, jnp.transpose(img_weight, (1, 0, 2)),
-        jnp.transpose(txt_weight, (1, 0, 2)), img_modulation, txt_modulation, feat, gains, live,
-        img_cotangent, txt_cotangent,
+        jnp.transpose(txt_weight, (1, 0, 2)), img_modulation, txt_modulation, features,
+        qk_gains.reshape(4, HD), valid_text, img_cotangent, txt_cotangent,
     )
+    shapes = tuple(jax.ShapeDtypeStruct(v.shape, v.dtype) for v in (dw_img, dw_txt, dx_img, dx_txt))
+    dw_img, dw_txt, dx_img, dx_txt = pl.pallas_call(
+        finish, out_shape=shapes, in_specs=[vm] * 4, out_specs=[vm] * 4, name="results",
+    )(dw_img, dw_txt, dx_img, dx_txt)
     return (
         jnp.transpose(dw_img, (1, 0, 2)), jnp.transpose(dw_txt, (1, 0, 2)), dx_img, dx_txt
     )

time: 177 us -> 128 us (0.72)
  Pallas kernels: 165 us -> 125 us
  local copies, waits for them, and re-layouts: 9.52 us -> 0 us
    pallas_call x1, Pallas kernels: 165 us -> 123 us  [on_device(): pl.pallas_call(kernel, out_shape=(jax.ShapeDtypeStruct((3, 192, 256), F32...]
    unnamed x4 -> x0, local copies, waits for them, and re-layouts: 6.8 us -> none
    pallas_call x0 -> x1, Pallas kernels: none -> 2.39 us  [on_device(): pl.pallas_call(finish, out_shape=shapes, in_specs=[vm] * 4, out_specs=[vm...]
where the time goes in v2:
time: 128 us
  Pallas kernels  125 us (98%)
  between operations  1.94 us (2%)
    pallas_call x1, Pallas kernels, on_device(): pl.pallas_call(kernel, out_shape=(jax.ShapeDtypeStruct((3, 192, 256), F32...  123 us

profile of v2, /device:TPU:1, one launch (start us, length us, event | category | flops | bytes accessed | tf_op | source)
XLA Modules:
  0.0 127.7 jit_solution(2964143337566073951)
XLA Ops:
  2.0 0.6 fusion.feat
  2.6 122.8 %joint_block.1 = (f32[3,192,256]{2,1,0:T(8,128)}, f32[3,192,256]{2,1,0:T(8,128)}, bf16[256,384]{1,0:T(8,128)(2,1)}, bf16[32,384]{1,0:T(8,128)(2,1)}) custom-call(bf16[256,3072]{1,0:T(8,128)(2,1)} %x_img.1, bf16[32,3072]{1,0:T(8,128)(2,1)} %x_txt.1, bf16[3,384,2048]{2,1,0:T(8,128)(2,1)} %bitcast.10, bf16[3,384,2048]{2,1,0:T(8,128)(2,1)} %bitcast.11, ...), custom_call_target="tpu_custom_call" | custom-call | tf_op jit(solution)/shard_map/joint_block/pallas_call | solution.py:633
  125.3 2.4 %results.1 = (f32[3,192,256]{2,1,0:T(8,128)}, f32[3,192,256]{2,1,0:T(8,128)}, bf16[256,384]{1,0:T(8,128)(2,1)}, bf16[32,384]{1,0:T(8,128)(2,1)}) custom-call(f32[3,192,256]{2,1,0:T(8,128)} %get-tuple-element.12.a, f32[3,192,256]{2,1,0:T(8,128)} %get-tuple-element.13.b, bf16[256,384]{1,0:T(8,128)(2,1)} %get-tuple-element.14.c, ...), custom_call_target="tpu_custom_call" | custom-call | tf_op jit(solution)/shard_map/results/pallas_call | solution.py:653
  (1 shorter events, 0.0 us)

commit v3 on v2

--- a/solution.py
+++ b/solution.py
@@ -50,7 +50,7 @@
     tps, tpr, qkvp, dO, qr, qT, dOT, q2, dO2, kv, kvt, ets, etx, dkvs, dkvr, dkvts, dkvtr,
     oT, stx, stxr, dqf, dqr, gq, gtf, gts, dws, dwr, pxs, pxr, phs, phr, s1v, s2v, sts, str_,
     thx, thr, tsts, tstr, wx, wxr, wxt, wxtr, wsum, wcs, wcr,
-    lsem, wl_sem, wtl_sem, w_ss, w_rs, p_ss, p_rs, x_ss, x_rs, t_ss, t_rs, h_ss, h_rs,
+    lsem, wl_sem, wtl_sem, w_ss, w_rs, z_ss, z_rs, p_ss, p_rs, x_ss, x_rs, t_ss, t_rs, h_ss, h_rs,
     kv_ss, kv_rs, kt_ss, kt_rs, dk_ss, dk_rs, dt_ss, dt_rs, gf_ss, gf_rs, gs_ss, gs_rs,
     dq_ss, dq_rs, dw_ss, dw_rs, ph_ss, ph_rs, st_ss, st_rs, ts_ss, ts_rs,
 ):
@@ -130,23 +130,44 @@
     for j in range(3):
         wl_copy(j).start()
 
-    pl.semaphore_wait(barrier, 15)
+    hz = z % 2
+    my_half = pl.ds(pl.multiple_of(hz * 192, 64), 192)
 
     def w_copy(r, j):
         return remote(
-            w_cols(w_img, j, f_at(r, 1)), W.at[r, :, pl.ds(j * 128, 128)],
-            w_ss.at[r, j], w_rs.at[r, j], fdev(r, 1))
+            w_img.at[j, my_half, pl.ds(m128((2 * f_at(r, 1) + c) * 128), 128)],
+            W.at[r, my_half, pl.ds(j * 128, 128)],
+            w_ss.at[r, j], w_rs.at[r, 1], fdev(r, 1))
+
+    def w_landed(r):
+        ref = W.at[r, my_half, pl.ds(128, 256)]
+        return remote(ref, ref, w_ss.at[r, 1], w_rs.at[r, 1], fdev(r, 1))
+
+    def wq_copy(r):
+        return remote(
+            w_cols(w_img, 0, f_at(r, 1)), W.at[r, :, pl.ds(0, 128)],
+            w_ss.at[r, 0], w_rs.at[r, 0], fdev(r, 1))
+
+    def z_copy(d, r, half):
+        ref = W.at[r, pl.ds(pl.multiple_of(half * 192 + d * 96, 32), 96), pl.ds(128, 256)]
+        return remote(ref, ref, z_ss.at[d, r], z_rs.at[d, r], sdev(1, 1 - 2 * d))
 
     def send_w(r):
-        for j in range(3):
+        for j in (1, 2):
             w_copy(r, j).start()
-
-    loop(1, 8, send_w)
 
     def start_wt(r):
         for j in range(3):
             wt_copy(r, j).start()
 
+    def pass_w(r):
+        w_landed(r).wait_recv()
+        for d in (0, 1):
+            z_copy(d, r, hz).start()
+        wq_copy(r).start()
+
+    pl.semaphore_wait(barrier, 15)
+    loop(1, 8, send_w)
     loop(0, 8, start_wt)
 
     img_rows = pl.ds(pl.multiple_of(128 + c * 256, 128), 256)
@@ -182,6 +203,8 @@
             for b in range(8):
                 nrm[b, pl.ds(at, rows), :] = n[:, b * 384:(b + 1) * 384]
                 put(b, at, rows, h[:, b * 384:(b + 1) * 384])
+            if which == 1:
+                pl.when((i > 4) & (i < 12))(lambda: pass_w(i - 4))
 
         loop(0, src.shape[0] // rows, body)
 
@@ -239,20 +262,11 @@
     qkvp[128:, :] = dot(hid[f], W[0])
 
     def img_proj(r):
-        for j in range(3):
-            w_copy(r, j).wait_recv()
-        qkvp[128:, :] += dot(hid[f_at(r, -1)], W[r])
+        for d in (0, 1):
+            z_copy(d, r, 1 - hz).wait_recv()
+        qkvp[128:, 128:384] += dot(hid[f_at(r, -1)], W[r, :, 128:384])
 
     loop(1, 8, img_proj)
-
-    qkvp[0:64, :] = tps[0].astype(F32)
-    qkvp[64:128, :] = jnp.zeros((64, 384), F32)
-
-    def txt_add(r):
-        t_copy(r).wait_recv()
-        qkvp[0:64, :] += tpr[r].astype(F32)
-
-    loop(1, 8, txt_add)
 
     def normed_head(lo, hi, col, g):
         a = qkvp[lo:hi, col:col + 128]
@@ -268,9 +282,23 @@
     kv[0, :, 0:128] = normed_head(128, 640, 128, 3)
     kv[0, :, 128:256] = qkvp[128:, 256:384].astype(BF)
     loop(1, 4, lambda r: kv_copy(r).start())
+
+    qkvp[0:64, :] = tps[0].astype(F32)
+
+    def txt_add(r):
+        t_copy(r).wait_recv()
+        qkvp[0:64, :] += tpr[r].astype(F32)
+
+    loop(1, 8, txt_add)
     kvt[0, :, 0:128] = normed_head(0, 64, 128, 1)
     kvt[0, :, 128:256] = qkvp[0:64, 256:384].astype(BF)
     loop(1, 4, lambda r: kt_copy(r).start())
+
+    def img_query(r):
+        wq_copy(r).wait_recv()
+        qkvp[128:, 0:128] += dot(hid[f_at(r, -1)], W[r, :, 0:128])
+
+    loop(1, 8, img_query)
     qr[own_i, :] = normed_head(128, 640, 0, 2)
     qr[own_t, :] = normed_head(0, 64, 0, 0)
     cp_xqt = remote(qr.at[own_t], qr.at[own_t], x_ss.at[2], x_rs.at[2], xdev)
@@ -467,6 +495,17 @@
 
     loop(0, 8, both)
 
+    def add_w(r):
+        dw_copy(r, 0).wait_recv()
+        dw_copy(r, 1).wait_recv()
+        wx[...] += dwr[r].astype(F32)
+
+    wx[...] = dws[4].astype(F32)
+    loop(5, 8, add_w)
+    wcs[...] = wx[...].astype(BF)
+    cp_wc = remote(wcs, wcr, x_ss.at[7], x_rs.at[7], xdev)
+    cp_wc.start()
+
     lane = lax.broadcasted_iota(jnp.int32, (256, 128), 1)
     s1 = jnp.sum(s1v[...], axis=-1, keepdims=True)
     s2 = jnp.sum(s2v[...], axis=-1, keepdims=True)
@@ -544,16 +583,6 @@
         thr[...] - tt[:, 0:1] * (1.0 / 3072) - ntxt[f] * (tt[:, 1:2] * (1.0 / 3072))
     )).astype(BF)
 
-    def add_w(r):
-        dw_copy(r, 0).wait_recv()
-        dw_copy(r, 1).wait_recv()
-        wx[...] += dwr[r].astype(F32)
-
-    wx[...] = dws[4].astype(F32)
-    loop(5, 8, add_w)
-    wcs[...] = wx[...].astype(BF)
-    cp_wc = remote(wcs, wcr, x_ss.at[7], x_rs.at[7], xdev)
-    cp_wc.start()
     wx[...] = dws[0].astype(F32)
     loop(1, 4, add_w)
     cp_wc.wait_recv()
@@ -565,8 +594,11 @@
     place(dw_img, wxr[...], o)
 
     def drain(r):
-        for j in range(3):
+        for j in (1, 2):
             w_copy(r, j).wait_send()
+        wq_copy(r).wait_send()
+        for d in (0, 1):
+            z_copy(d, r, hz).wait_send()
         for cp in (t_copy, h_copy, gf_copy, gs_copy, ph_copy, st_copy, ts_copy):
             cp(r).wait_send()
 
@@ -617,7 +649,7 @@
     ] + [
         pltpu.SemaphoreType.DMA(shape)
         for shape in (
-            [(6,), (3,), (8, 3), (8, 3), (8, 3), (7,), (7,), (8,), (8,)] + [(8,)] * 4
+            [(6,), (3,), (8, 3), (8, 3), (8, 2), (2, 8), (2, 8), (7,), (7,), (8,), (8,)] + [(8,)] * 4
             + [(4,)] * 8 + [(8,)] * 8 + [(2, 8)] * 2 + [(8,)] * 4
         )
     ]

time: 128 us -> 120 us (0.938)
  Pallas kernels: 125 us -> 118 us
    pallas_call x1, Pallas kernels: 123 us -> 115 us  [on_device(): pl.pallas_call(kernel, out_shape=(jax.ShapeDtypeStruct((3, 192, 256), F32...]
where the time goes in v3:
time: 120 us
  Pallas kernels  118 us (98%)
  between operations  1.94 us (2%)
    pallas_call x1, Pallas kernels, on_device(): pl.pallas_call(kernel, out_shape=(jax.ShapeDtypeStruct((3, 192, 256), F32...  115 us

profile of v3, /device:TPU:1, one launch (start us, length us, event | category | flops | bytes accessed | tf_op | source)
XLA Modules:
  0.0 120.3 jit_solution(587768760642174605)
XLA Ops:
  2.0 0.6 fusion.feat
  2.6 115.3 %joint_block.1 = (f32[3,192,256]{2,1,0:T(8,128)}, f32[3,192,256]{2,1,0:T(8,128)}, bf16[256,384]{1,0:T(8,128)(2,1)}, bf16[32,384]{1,0:T(8,128)(2,1)}) custom-call(bf16[256,3072]{1,0:T(8,128)(2,1)} %x_img.1, bf16[32,3072]{1,0:T(8,128)(2,1)} %x_txt.1, bf16[3,384,2048]{2,1,0:T(8,128)(2,1)} %bitcast.10, bf16[3,384,2048]{2,1,0:T(8,128)(2,1)} %bitcast.11, ...), custom_call_target="tpu_custom_call" | custom-call | tf_op jit(solution)/shard_map/joint_block/pallas_call | solution.py:665
  117.9 2.4 %results.1 = (f32[3,192,256]{2,1,0:T(8,128)}, f32[3,192,256]{2,1,0:T(8,128)}, bf16[256,384]{1,0:T(8,128)(2,1)}, bf16[32,384]{1,0:T(8,128)(2,1)}) custom-call(f32[3,192,256]{2,1,0:T(8,128)} %get-tuple-element.12.a, f32[3,192,256]{2,1,0:T(8,128)} %get-tuple-element.13.b, bf16[256,384]{1,0:T(8,128)(2,1)} %get-tuple-element.14.c, ...), custom_call_target="tpu_custom_call" | custom-call | tf_op jit(solution)/shard_map/results/pallas_call | solution.py:685
  (1 shorter events, 0.0 us)

commit v4 on v1

v4 whole, which is shorter than its diff:
```python
import functools
import math

import jax
import jax.numpy as jnp
from jax import lax
from jax.experimental import pallas as pl
from jax.experimental.pallas import tpu as pltpu
from jax.sharding import PartitionSpec as P

HD = 128
BF = jnp.bfloat16
F32 = jnp.float32
MESH = pl.DeviceIdType.MESH
SCALE = HD ** (-0.5)
EXP2 = SCALE / math.log(2.0)
EPS = 1e-06


def time_features(timestep, freq_dim):
    half_freq = freq_dim // 2
    frequency = jnp.exp(-math.log(10000.0) * jnp.arange(half_freq, dtype=jnp.float32) / half_freq)
    angles = timestep.astype(jnp.float32)[:, None] * frequency[None, :]
    features = jnp.concatenate([jnp.cos(angles), jnp.sin(angles)], axis=1)
    return jax.nn.silu(features).astype(jnp.bfloat16)


def dot(a, b):
    return jnp.dot(a, b, preferred_element_type=F32)


def dot_nt(a, b):
    return lax.dot_general(a, b, (((1,), (1,)), ((), ())), preferred_element_type=F32)


def dot_tn(a, b):
    return lax.dot_general(a, b, (((0,), (0,)), ((), ())), preferred_element_type=F32)


def norm_back(x, gain, grad):
    r = lax.rsqrt(jnp.mean(x * x, axis=-1, keepdims=True) + EPS)
    gd = gain * grad
    return r * gd - x * (r * r * r * jnp.mean(x * gd, axis=-1, keepdims=True))


def kernel(
    x_img, x_txt, w_img, w_txt, mod_img, mod_txt, feat, gains, valid, cot_img, cot_txt,
    dw_img, dw_txt, dx_img, dx_txt,
    xi, xt, mods, mixed, sc, W, wt, hid, hidt, htg, nimg, ntxt, invi, invt,
    tps, tpr, qkvp, dO, qr, qT, dOT, q2, dO2, kv, ets, acc, dks, dkr,
    dqT, stx, stxr, stf, dqs, dqr, dqts, dqtr, gq, gtf, gts, dws, dwr, rl, pxs, pxr, phs, phr,
    hcs, hcr, s1v, s2v, sts, str_,
    thx, thr, tsts, tstr, wx, wxr, wxt, wxtr, wcs, wcr,
    lsem, wl_sem, wtl_sem, w_ss, w_rs, z_ss, z_rs, p_ss, p_rs, x_ss, x_rs, t_ss, t_rs, h_ss, h_rs,
    do_ss, do_rs, q_ss, q_rs, dq_ss, dq_rs, sx_ss, sx_rs, rl_ss, rl_rs,
    gf_ss, gf_rs, gs_ss, gs_rs, dw_ss, dw_rs, ph_ss, ph_rs, st_ss, st_rs, ts_ss, ts_rs,
):
    s = lax.axis_index("seq")
    f = lax.axis_index("fsdp")
    chip, c = s // 2, s % 2
    xlo, z = chip // 4, chip % 4
    y, xhi = f // 2, f % 2
    o = 1 - c

    def f_at(r, sign):
        return ((y + sign * (r % 4) + 4) % 4) * 2 + (xhi + r // 4) % 2

    def chip_at(r, sign):
        return ((xlo + r // 4) % 2) * 4 + (z + sign * (r % 4) + 4) % 4

    def fdev(r, sign):
        return (s, f_at(r, sign))

    def sdev(r, sign):
        return (chip_at(r, sign) * 2 + c, f)

    pdev = (chip * 2 + o, f)
    xdev = sdev(4, 1)
    xo = 1 - xlo
    xodev = ((xo * 4 + z) * 2 + o, f)

    def remote(src, dst, ss, rs, dev):
        return pltpu.make_async_remote_copy(
            src_ref=src, dst_ref=dst, send_sem=ss, recv_sem=rs, device_id=dev, device_id_type=MESH
        )

    def loop(lo, hi, body):
        def step(i, carry):
            body(i)
            return carry

        lax.fori_loop(lo, hi, step, 0)

    def m128(v):
        return pl.multiple_of(v, 128)

    loc = [
        pltpu.make_async_copy(x_img, xi, lsem.at[0]),
        pltpu.make_async_copy(x_txt, xt, lsem.at[1]),
        pltpu.make_async_copy(mod_img, mods.at[1], lsem.at[2]),
        pltpu.make_async_copy(mod_txt, mods.at[0], lsem.at[3]),
        pltpu.make_async_copy(
            cot_img.at[:, pl.ds(m128(c * 128), 128)],
            dO.at[pl.ds(pl.multiple_of(z * 512 + c * 256, 256), 256)], lsem.at[4]),
        pltpu.make_async_copy(
            cot_txt.at[:, pl.ds(m128(c * 128), 128)],
            dO.at[pl.ds(pl.multiple_of(2048 + z * 64 + c * 32, 32), 32)], lsem.at[5]),
    ]
    for cp in loc:
        cp.start()

    barrier = pltpu.get_barrier_semaphore()

    def hello(r):
        pl.semaphore_signal(barrier, inc=1, device_id=fdev(r, 1), device_id_type=MESH)
        pl.semaphore_signal(barrier, inc=1, device_id=sdev(r, 1), device_id_type=MESH)

    loop(1, 8, hello)
    pl.semaphore_signal(barrier, inc=1, device_id=pdev, device_id_type=MESH)
    pl.semaphore_signal(barrier, inc=1, device_id=xodev, device_id_type=MESH)

    def w_cols(ref, j, fp):
        return ref.at[j, :, pl.ds(m128((2 * fp + c) * 128), 128)]

    def wl_copy(j):
        return pltpu.make_async_copy(
            w_cols(w_img, j, f), W.at[0, :, pl.ds(j * 128, 128)], wl_sem.at[j])

    def wt_copy(r, j):
        return pltpu.make_async_copy(
            w_cols(w_txt, j, f_at(r, 1)), wt.at[r, :, pl.ds(j * 128, 128)], wtl_sem.at[r, j])

    for j in range(3):
        wl_copy(j).start()

    hz = z % 2
    my_half = pl.ds(pl.multiple_of(hz * 192, 64), 192)

    def w_copy(r, j):
        return remote(
            w_img.at[j, my_half, pl.ds(m128((2 * f_at(r, 1) + c) * 128), 128)],
            W.at[r, my_half, pl.ds(j * 128, 128)],
            w_ss.at[r, j], w_rs.at[r, j], fdev(r, 1))

    def wv_copy(r):
        return remote(
            w_cols(w_img, 2, f_at(r, 1)), W.at[r, :, pl.ds(256, 128)],
            w_ss.at[r, 2], w_rs.at[r, 2], fdev(r, 1))

    def z_copy(j, d, r, half):
        ref = W.at[r, pl.ds(pl.multiple_of(half * 192 + d * 96, 32), 96), pl.ds(j * 128, 128)]
        return remote(ref, ref, z_ss.at[j, d, r], z_rs.at[j, d, r], sdev(1, 1 - 2 * d))

    def start_wt(r):
        for j in range(3):
            wt_copy(r, j).start()

    def pass_w(j):
        def one(r):
            w_copy(r, j).wait_recv()
            for d in (0, 1):
                z_copy(j, d, r, hz).start()

        loop(1, 8, one)

    def start_keys():
        loop(1, 8, lambda r: w_copy(r, 0).wait_send())
        loop(1, 8, lambda r: w_copy(r, 1).start())

    pl.semaphore_wait(barrier, 16)
    loop(1, 8, lambda r: w_copy(r, 0).start())
    loop(0, 8, start_wt)

    img_rows = pl.ds(pl.multiple_of(128 + c * 256, 128), 256)
    txt_rows = pl.ds(pl.multiple_of(c * 32, 32), 32)
    half_rows = pl.ds(pl.multiple_of(c * 256, 256), 256)
    cp_coti = remote(cot_img.at[:, pl.ds(m128(o * 128), 128)],
                     dO.at[pl.ds(pl.multiple_of(z * 512 + c * 256, 256), 256)],
                     p_ss.at[0], p_rs.at[0], pdev)
    cp_cott = remote(cot_txt.at[:, pl.ds(m128(o * 128), 128)],
                     dO.at[pl.ds(pl.multiple_of(2048 + z * 64 + c * 32, 32), 32)],
                     p_ss.at[1], p_rs.at[1], pdev)
    cp_coti.start()
    cp_cott.start()

    for which in (0, 1):
        loc[3 - which].wait()
        row = jnp.broadcast_to(feat[...].astype(F32), (16, 256)).astype(BF)
        mixed[which] = dot(row, mods[which])[:8]
        for b in range(8):
            sc[which, b] = 1.0 + mixed[which, :, 3072 + b * 384:3072 + (b + 1) * 384]

    def z_rows(part, zz):
        if part == 0:
            return pl.ds(pl.multiple_of(zz * 512, 512), 512)
        return pl.ds(pl.multiple_of(2048 + zz * 64, 64), 64)

    def ring_copy(ref, ss, rs, part, b, zz):
        rows = ref.at[z_rows(part, zz)]
        return remote(rows, rows, ss.at[part, b], rs.at[part, b], sdev(b, 1))

    def z_back(b):
        return (z + 4 - b) % 4

    loc[4].wait()
    loc[5].wait()
    cp_coti.wait_recv()
    cp_cott.wait_recv()

    def send_do(b):
        for part in (0, 1):
            ring_copy(dO, do_ss, do_rs, part, b, z).start()

    loop(1, 4, send_do)

    def prepare(which, src, nrm, inv, put):
        rows = 16

        def body(i):
            at = pl.multiple_of(i * rows, rows)
            v = src[pl.ds(at, rows), :].astype(F32)
            cen = v - jnp.mean(v, axis=-1, keepdims=True)
            iv = lax.rsqrt(jnp.mean(cen * cen, axis=-1, keepdims=True) + EPS)
            n = cen * iv
            inv[pl.ds(at, rows), :] = jnp.broadcast_to(iv, (rows, 128))
            h = (n * (1.0 + mixed[which, 0:1, 3072:]) + mixed[which, 0:1, :3072]).astype(BF)
            for b in range(8):
                nrm[b, pl.ds(at, rows), :] = n[:, b * 384:(b + 1) * 384]
                put(b, at, rows, h[:, b * 384:(b + 1) * 384])
            if which == 1:
                pl.when(i == 8)(start_keys)

        loop(0, src.shape[0] // rows, body)

    def put_txt(b, at, rows, h):
        hidt[b, pl.ds(pl.multiple_of(c * 32 + at, 16), rows), :] = h

    def put_img(b, at, rows, h):
        hid[b, pl.ds(pl.multiple_of(c * 256 + at, 16), rows), :] = h

    loc[1].wait()
    prepare(0, xt, ntxt, invt, put_txt)
    cp_ht = remote(hidt.at[:, txt_rows], hidt.at[:, txt_rows], p_ss.at[2], p_rs.at[2], pdev)
    cp_ht.start()
    loc[0].wait()
    prepare(1, xi, nimg, invi, put_img)
    cp_hi = remote(hid.at[:, half_rows], hid.at[:, half_rows], p_ss.at[3], p_rs.at[3], pdev)
    cp_hi.start()

    pass_w(0)
    loop(1, 8, lambda r: w_copy(r, 1).wait_send())
    loop(1, 8, lambda r: wv_copy(r).start())

    cp_ht.wait_recv()

    def t_copy(r):
        return remote(tps.at[r], tpr.at[r], t_ss.at[r], t_rs.at[r], fdev(r, 1))

    def h_copy(r):
        return remote(hidt.at[chip_at(r, 1)], htg.at[r], h_ss.at[r], h_rs.at[r], sdev(r, 1))

    def txt_partial(i):
        r = (i + 1) % 8
        for j in range(3):
            wt_copy(r, j).wait()
        tps[r] = dot(hidt[f], wt[r]).astype(BF)

        @pl.when(r != 0)
        def _():
            t_copy(r).start()

    loop(0, 8, txt_partial)
    pass_w(1)

    def normed_head(lo, hi, col, g):
        a = qkvp[lo:hi, col:col + 128]
        return (a * lax.rsqrt(jnp.mean(a * a, axis=-1, keepdims=True) + EPS)
                * gains[g:g + 1, :]).astype(BF)

    def kv_copy(lo, n, col, wide, at):
        cols = pl.ds(col, wide)
        return remote(kv.at[pl.ds(lo, n), cols], kv.at[pl.ds(lo + 576, n), cols],
                      x_ss.at[at], x_rs.at[at], xdev)

    cp_kvk = kv_copy(0, 512, 0, 128, 0)
    cp_kvv = kv_copy(0, 512, 128, 128, 5)
    cp_kvt = kv_copy(512, 64, 0, 256, 1)

    def send_q(part):
        loop(1, 4, lambda b: ring_copy(qr, q_ss, q_rs, part, b, z).start())

    def project(j):
        lo, hi = j * 128, j * 128 + 128

        def one(r):
            if j == 2:
                wv_copy(r).wait_recv()
            else:
                for d in (0, 1):
                    z_copy(j, d, r, 1 - hz).wait_recv()
            qkvp[128:, lo:hi] += dot(hid[f_at(r, -1)], W[r, :, lo:hi])

        loop(1, 8, one)

    cp_hi.wait_recv()
    for j in range(3):
        wl_copy(j).wait()
    qkvp[128:, :] = dot(hid[f], W[0])
    project(0)
    qr[z_rows(0, z), :] = normed_head(128, 640, 0, 2)
    send_q(0)
    project(1)
    kv[0:512, 0:128] = normed_head(128, 640, 128, 3)
    cp_kvk.start()

    qkvp[0:64, :] = tps[0].astype(F32)

    def txt_add(r):
        t_copy(r).wait_recv()
        qkvp[0:64, :] += tpr[r].astype(F32)

    loop(1, 8, txt_add)
    kv[512:576, 0:128] = normed_head(0, 64, 128, 1)
    kv[512:576, 128:256] = qkvp[0:64, 256:384].astype(BF)
    cp_kvt.start()
    qr[z_rows(1, z), :] = normed_head(0, 64, 0, 0)
    send_q(1)
    project(2)
    kv[0:512, 128:256] = qkvp[128:, 256:384].astype(BF)
    cp_kvv.start()

    def wait_do(b):
        for part in (0, 1):
            ring_copy(dO, do_ss, do_rs, part, b, z_back(b)).wait_recv()

    loop(1, 4, wait_do)
    dOT[...] = dO[...].astype(F32).T.astype(BF)

    def cols_at(i):
        return pl.ds(pl.multiple_of(i * 256, 256), 256)

    def chunk_at(i):
        return ((z + i // 2) % 4) * 2 + i % 2

    def forward(idx):
        cols = cols_at(idx)
        tot = jnp.zeros((1, 256), F32)
        for a in (0, 1):
            e = jnp.exp2(dot(kv[a * 576:a * 576 + 576, 0:128], qT[:, cols]) * EXP2)
            index = chip_at(a * 4, 1) * 64 + lax.broadcasted_iota(jnp.int32, (64, 256), 0)
            et = jnp.where(index < valid[0], e[512:576], 0.0)
            tot += jnp.sum(e[0:512], axis=0, keepdims=True) + jnp.sum(et, axis=0, keepdims=True)
            ets[idx, a * 576:a * 576 + 512, :] = e[0:512].astype(BF)
            ets[idx, a * 576 + 512:a * 576 + 576, :] = et.astype(BF)
        part = dot_tn(kv[:, 128:256], ets[idx])
        stx[0:1, cols] = tot
        stx[1:2, cols] = jnp.sum(dOT[:, cols].astype(F32) * part, axis=0, keepdims=True)

    cp_kvk.wait_recv()
    cp_kvt.wait_recv()
    cp_kvv.wait_recv()

    def forward_img(k):
        b = (4 - k) % 4

        @pl.when(b != 0)
        def _():
            ring_copy(qr, q_ss, q_rs, 0, b, z_back(b)).wait_recv()

        zz = z_back(b)
        rows = z_rows(0, zz)
        qT[:, rows] = qr[rows, :].astype(F32).T.astype(BF)
        loop(0, 2, lambda h: forward(zz * 2 + h))

    loop(0, 4, forward_img)
    loop(1, 4, lambda b: ring_copy(qr, q_ss, q_rs, 1, b, z_back(b)).wait_recv())
    qT[:, 2048:2304] = qr[2048:2304, :].astype(F32).T.astype(BF)
    forward(8)

    def sx_copy(b):
        return remote(stx, stxr.at[b], sx_ss.at[b], sx_rs.at[b], sdev(b, 1))

    loop(1, 4, lambda b: sx_copy(b).start())
    loop(1, 4, lambda b: sx_copy(b).wait_recv())
    sums = stx[...] + stxr[1] + stxr[2] + stxr[3]
    rcp = 1.0 / sums[0:1]
    stf[0:1, :] = rcp
    stf[1:2, :] = sums[1:2] * rcp
    q2[...] = (qT[...].astype(F32) * rcp).T.astype(BF)
    dO2[...] = (dOT[...].astype(F32) * rcp).T.astype(BF)
    htg[0] = hidt[chip]
    loop(1, 8, lambda r: h_copy(r).start())

    def back(a, idx):
        cols = cols_at(idx)
        keys = slice(a * 576, a * 576 + 576)
        dp = dot(kv[keys, 128:256], dOT[:, cols])
        eb = ets[idx, keys, :]
        ds = (eb.astype(F32) * (dp - stf[1:2, cols])).astype(BF)
        part = dot_tn(kv[keys, 0:128], ds)
        if a == 1:
            dqT[:, cols] = part
        else:
            dqT[:, cols] += part
        acc[:, 0:128] += dot(ds, q2[cols, :])
        acc[:, 128:256] += dot(eb, dO2[cols, :])

    acc[...] = jnp.zeros_like(acc)
    loop(0, 9, lambda i: back(1, i))
    dks[:, 0:128] = (acc[:, 0:128] * SCALE).astype(BF)
    dks[:, 128:256] = acc[:, 128:256].astype(BF)
    cp_dk = remote(dks, dkr, x_ss.at[2], x_rs.at[2], xdev)
    cp_dk.start()
    acc[...] = jnp.zeros_like(acc)

    def dq_rows(cols):
        return (dqT[:, cols] * (stf[0:1, cols] * SCALE)).T

    def dq_copy(b):
        return remote(dqs.at[b], dqr.at[b], dq_ss.at[0, b], dq_rs.at[0, b], sdev(b, 1))

    def dqt_copy(b):
        mine = pl.ds(pl.multiple_of(((z + b) % 4) * 64, 64), 64)
        return remote(dqts.at[mine], dqtr.at[b], dq_ss.at[1, b], dq_rs.at[1, b], sdev(b, 1))

    def back_peer(b):
        zz = (z + b) % 4
        loop(0, 2, lambda h: back(0, zz * 2 + h))
        dqs[b] = dq_rows(z_rows(0, zz)).astype(BF)
        dq_copy(b).start()

    loop(1, 4, back_peer)
    back(0, 8)
    dqts[...] = dq_rows(slice(2048, 2304)).astype(BF)
    loop(1, 4, lambda b: dqt_copy(b).start())
    loop(0, 2, lambda h: back(0, z * 2 + h))

    cp_dk.wait_recv()
    acc[:, 0:128] = acc[:, 0:128] * SCALE + dkr[:, 0:128].astype(F32)
    acc[:, 128:256] += dkr[:, 128:256].astype(F32)
    gq[128:, 128:256] = norm_back(
        qkvp[128:, 128:256], gains[3:4, :], acc[0:512, 0:128]).astype(BF)
    gq[128:, 256:384] = acc[0:512, 128:256].astype(BF)
    gq[0:64, 128:256] = norm_back(
        qkvp[0:64, 128:256], gains[1:2, :], acc[512:576, 0:128]).astype(BF)
    gq[0:64, 256:384] = acc[512:576, 128:256].astype(BF)

    dqi = dq_rows(z_rows(0, z))
    own_text = pl.ds(pl.multiple_of(z * 64, 64), 64)
    for b in (1, 2, 3):
        dqt_copy(b).wait_recv()
    dqt = dqts[own_text, :].astype(F32)
    for b in (1, 2, 3):
        dqt = dqt + dqtr[b].astype(F32)
    gq[0:64, 0:128] = norm_back(qkvp[0:64, 0:128], gains[0:1, :], dqt).astype(BF)
    for b in (1, 2, 3):
        dq_copy(b).wait_recv()
        dqi = dqi + dqr[b].astype(F32)
    gq[128:, 0:128] = norm_back(qkvp[128:, 0:128], gains[2:3, :], dqi).astype(BF)

    def gf_copy(r):
        return remote(gtf.at[0], gtf.at[r], gf_ss.at[r], gf_rs.at[r], fdev(r, 1))

    def gs_copy(r):
        return remote(gts.at[0], gts.at[r], gs_ss.at[r], gs_rs.at[r], sdev(r, 1))

    gtf[0] = gq[0:64, :]
    gts[0] = gq[0:64, :]
    loop(1, 8, lambda r: gf_copy(r).start())

    def dw_block(a, b):
        return dot_tn(hid[chip_at(a * 4 + b, 1)], gq[128:, :])

    def rl_copy(a, d):
        rows = pl.ds(d * 192, 192)
        return remote(dws.at[a * 4 + 2, rows], rl.at[a, rows], rl_ss.at[a, d], rl_rs.at[a, d],
                      sdev(1 + 2 * d, 1))

    def dw_copy(r):
        return remote(dws.at[r], dwr.at[r], dw_ss.at[r], dw_rs.at[r], sdev(r % 4, 1))

    dws[6] = dw_block(1, 2).astype(BF)
    for d in (0, 1):
        rl_copy(1, d).start()
    dws[2] = dw_block(0, 2).astype(BF)

    other_rows = pl.ds(pl.multiple_of(128 + o * 256, 128), 256)

    def px_copy(r):
        return remote(pxs.at[r], pxr.at[r], ph_ss.at[0, r], ph_rs.at[0, r], pdev)

    def partner_part(i):
        r = (7 - i) % 8
        pxs[r] = dot_nt(gq[other_rows, :], W[r]).astype(BF)
        px_copy(r).start()

    loop(0, 8, partner_part)
    for d in (0, 1):
        rl_copy(1, d).wait_send()
    for d in (0, 1):
        rl_copy(0, d).start()

    def ph_copy(r):
        return remote(phs.at[r], phr.at[r], ph_ss.at[1, r], ph_rs.at[1, r], fdev(r % 4, -1))

    s1v[...] = jnp.zeros_like(s1v)
    s2v[...] = jnp.zeros_like(s2v)

    def hidden_part(i):
        r = (7 - i) % 8
        b = f_at(r, -1)
        px_copy(r).wait_recv()
        p = (dot_nt(gq[img_rows, :], W[r]) + pxr[r].astype(F32)).astype(BF)
        phs[r] = p

        @pl.when(r % 4 != 0)
        def _():
            ph_copy(r).start()

        t = p.astype(F32) * sc[1, b, 0:1, :]
        u = t * nimg[b]
        s1v[...] += t[:, 0:128] + t[:, 128:256] + t[:, 256:384]
        s2v[...] += u[:, 0:128] + u[:, 128:256] + u[:, 256:384]

    def passed_on(a, d):
        rl_copy(a, d).wait_recv()
        r = a * 4 + 1 + 2 * d
        block = dw_block(a, 1 + 2 * d)
        lo, hi = d * 192, d * 192 + 192
        dws[r, 192 - lo:384 - lo, :] = block[192 - lo:384 - lo].astype(BF)
        dws[r, lo:hi, :] = (block[lo:hi] + rl[a, lo:hi, :].astype(F32)).astype(BF)

    loop(0, 2, hidden_part)
    for d in (0, 1):
        passed_on(1, d)
        dw_copy(5 + 2 * d).start()
    loop(2, 6, hidden_part)
    for d in (0, 1):
        passed_on(0, d)
    for d in (0, 1):
        dw_copy(5 + 2 * d).wait_send()
    for d in (0, 1):
        dw_copy(1 + 2 * d).start()
    loop(1, 8, lambda r: gs_copy(r).start())
    loop(6, 8, hidden_part)

    lane = lax.broadcasted_iota(jnp.int32, (256, 128), 1)
    s1 = jnp.sum(s1v[...], axis=-1, keepdims=True)
    s2 = jnp.sum(s2v[...], axis=-1, keepdims=True)
    sts[...] = jnp.where(lane == 0, s1, s2).T[0:8]

    def st_copy(r):
        return remote(sts, str_.at[r], st_ss.at[r], st_rs.at[r], fdev(r, 1))

    loop(1, 8, lambda r: st_copy(r).start())

    thx[...] = jnp.zeros_like(thx)

    def txt_hidden(r):
        @pl.when(r != 0)
        def _():
            gf_copy(r).wait_recv()

        thx[...] += dot_nt(gtf[r], wt[(r // 4) * 4 + (4 - r % 4) % 4])

    loop(0, 8, txt_hidden)
    their = pl.ds(pl.multiple_of(o * 32, 32), 32)
    cp_th = remote(thx.at[their], thr, p_ss.at[4], p_rs.at[4], pdev)
    cp_th.start()

    cp_th.wait_recv()
    gh = thx[txt_rows, :] + thr[...]
    tsc = gh * sc[0, f, 0:1, :]
    tn = ntxt[f]
    t1 = jnp.sum(tsc, axis=-1, keepdims=True)
    t2 = jnp.sum(tsc * tn, axis=-1, keepdims=True)
    lane_t = lax.broadcasted_iota(jnp.int32, (32, 128), 1)
    tsts[...] = jnp.where(lane_t == 0, t1, t2)

    def ts_copy(r):
        return remote(tsts, tstr.at[r], ts_ss.at[r], ts_rs.at[r], fdev(r, 1))

    loop(1, 8, lambda r: ts_copy(r).start())
    thr[...] = tsc

    mine = pl.ds(pl.multiple_of(c * 192, 64), 192)
    theirs = pl.ds(pl.multiple_of(o * 192, 64), 192)
    wx[...] = dw_block(1, 0)
    for r in (5, 7):
        dw_copy(r).wait_recv()
        wx[...] += dwr[r].astype(F32)
    wcs[...] = wx[...].astype(BF)
    cp_wc = remote(wcs.at[mine], wcr.at[0], x_ss.at[3], x_rs.at[3], xdev)
    cp_wo = remote(wcs.at[theirs], wcr.at[1], x_ss.at[6], x_rs.at[6], xodev)
    cp_wc.start()
    cp_wo.start()
    hsum = phs[4].astype(F32)
    for r in (5, 6, 7):
        ph_copy(r).wait_recv()
        hsum = hsum + phr[r].astype(F32)
    hcs[...] = hsum.astype(BF)
    cp_hc = remote(hcs, hcr, x_ss.at[4], x_rs.at[4], fdev(4, 1))
    cp_hc.start()
    wx[...] = dw_block(0, 0)

    loop(1, 8, lambda r: gs_copy(r).wait_recv())
    loop(1, 8, lambda r: h_copy(r).wait_recv())
    wxt[...] = dot_tn(htg[...].reshape(512, 384), gts[...].reshape(512, 384))
    cp_wt = remote(wxt.at[theirs], wxtr, p_ss.at[5], p_rs.at[5], pdev)
    cp_wt.start()

    def place(out, part, head):
        for j in range(3):
            out[j, :, pl.ds(m128(head * 128), 128)] = part[:, j * 128:(j + 1) * 128]

    for r in (1, 3):
        dw_copy(r).wait_recv()
        wx[...] += dwr[r].astype(F32)
    cp_wi = remote(wx.at[theirs], wxr, p_ss.at[6], p_rs.at[6], pdev)
    cp_wi.start()

    st = sts[...]
    for r in range(1, 8):
        st_copy(r).wait_recv()
        st = st + str_[r]
    stT = jnp.concatenate([st, jnp.zeros((120, 256), F32)], axis=0).T
    gsum = phs[0].astype(F32)
    for r in (1, 2, 3):
        ph_copy(r).wait_recv()
        gsum = gsum + phr[r].astype(F32)
    cp_hc.wait_recv()
    gsum = gsum + hcr[...].astype(F32)
    scaled = gsum * sc[1, f, 0:1, :]
    dx_img[...] = (invi[:, 0:1] * (
        scaled - stT[:, 0:1] * (1.0 / 3072) - nimg[f] * (stT[:, 1:2] * (1.0 / 3072))
    )).astype(BF)

    tt = tsts[...]
    for r in range(1, 8):
        ts_copy(r).wait_recv()
        tt = tt + tstr[r]
    dx_txt[...] = (invt[:, 0:1] * (
        thr[...] - tt[:, 0:1] * (1.0 / 3072) - ntxt[f] * (tt[:, 1:2] * (1.0 / 3072))
    )).astype(BF)

    cp_wt.wait_recv()
    place(dw_txt, wxt[mine, :], c)
    place(dw_txt, wxtr[...], o)
    cp_wc.wait_recv()
    place(dw_img, wx[mine, :] + wcr[0].astype(F32), c)
    cp_wi.wait_recv()
    cp_wo.wait_recv()
    place(dw_img, wxr[...] + wcr[1].astype(F32), o)

    def drain(r):
        wv_copy(r).wait_send()
        for j in (0, 1):
            for d in (0, 1):
                z_copy(j, d, r, hz).wait_send()
        for cp in (t_copy, h_copy, gf_copy, gs_copy, st_copy, ts_copy):
            cp(r).wait_send()

        @pl.when(r % 4 != 0)
        def _():
            ph_copy(r).wait_send()

    def drain_z(b):
        for part in (0, 1):
            ring_copy(dO, do_ss, do_rs, part, b, z).wait_send()
            ring_copy(qr, q_ss, q_rs, part, b, z).wait_send()
        for cp in (sx_copy, dq_copy, dqt_copy):
            cp(b).wait_send()

    loop(1, 8, drain)
    loop(1, 4, drain_z)
    loop(0, 8, lambda r: px_copy(r).wait_send())
    for d in (0, 1):
        rl_copy(0, d).wait_send()
        dw_copy(1 + 2 * d).wait_send()
    for cp in (cp_coti, cp_cott, cp_ht, cp_hi, cp_th, cp_wt, cp_wi, cp_kvk, cp_kvv, cp_kvt,
               cp_dk, cp_wc, cp_wo, cp_hc):
        cp.wait_send()


def finish(a, b, c, d, oa, ob, oc, od):
    oa[...] = a[...]
    ob[...] = b[...]
    oc[...] = c[...]
    od[...] = d[...]


def scratch():
    V = pltpu.VMEM
    return [
        V((256, 3072), BF), V((32, 3072), BF), V((2, 256, 6144), BF), V((2, 8, 6144), F32),
        V((2, 8, 8, 384), F32), V((8, 384, 384), BF), V((8, 384, 384), BF),
        V((8, 512, 384), BF), V((8, 64, 384), BF), V((8, 64, 384), BF),
        V((8, 256, 384), F32), V((8, 32, 384), F32), V((256, 128), F32), V((32, 128), F32),
        V((8, 64, 384), BF), V((8, 64, 384), BF), V((640, 384), F32), V((2304, 128), BF),
        V((2304, 128), BF), V((128, 2304), BF), V((128, 2304), BF), V((2304, 128), BF),
        V((2304, 128), BF),
        V((1152, 256), BF), V((9, 1152, 256), BF), V((576, 256), F32), V((576, 256), BF),
        V((576, 256), BF),
        V((128, 2304), F32), V((2, 2304), F32), V((4, 2, 2304), F32), V((2, 2304), F32),
        V((4, 512, 128), BF), V((4, 512, 128), BF), V((256, 128), BF), V((4, 64, 128), BF),
        V((640, 384), BF),
        V((8, 64, 384), BF), V((8, 64, 384), BF), V((8, 384, 384), BF), V((8, 384, 384), BF),
        V((2, 384, 384), BF),
        V((8, 256, 384), BF), V((8, 256, 384), BF), V((8, 256, 384), BF), V((8, 256, 384), BF),
        V((256, 384), BF), V((256, 384), BF),
        V((256, 128), F32), V((256, 128), F32), V((8, 256), F32), V((8, 8, 256), F32),
        V((64, 384), F32), V((32, 384), F32), V((32, 128), F32), V((8, 32, 128), F32),
        V((384, 384), F32), V((192, 384), F32), V((384, 384), F32), V((192, 384), F32),
        V((384, 384), BF), V((2, 192, 384), BF),
    ] + [
        pltpu.SemaphoreType.DMA(shape)
        for shape in (
            [(6,), (3,), (8, 3), (8, 3), (8, 3), (2, 2, 8), (2, 2, 8), (7,), (7,), (7,), (7,)]
            + [(8,)] * 4 + [(2, 4)] * 6 + [(4,)] * 2 + [(2, 2)] * 2 + [(8,)] * 6
            + [(2, 8)] * 2 + [(8,)] * 4
        )
    ]


def on_device(
    img_tokens, txt_tokens, img_weight, txt_weight, img_modulation, txt_modulation, qk_gains,
    timestep, valid_text, img_cotangent, txt_cotangent,
):
    features = time_features(timestep, img_modulation.shape[0])
    anys = pl.BlockSpec(memory_space=pl.ANY)
    vm = pl.BlockSpec(memory_space=pltpu.VMEM)
    dw_img, dw_txt, dx_img, dx_txt = pl.pallas_call(
        kernel,
        out_shape=(
            jax.ShapeDtypeStruct((3, 192, 256), F32),
            jax.ShapeDtypeStruct((3, 192, 256), F32),
            jax.ShapeDtypeStruct((256, 384), BF),
            jax.ShapeDtypeStruct((32, 384), BF),
        ),
        in_specs=[anys] * 6 + [vm] * 2 + [pl.BlockSpec(memory_space=pltpu.SMEM)] + [anys] * 2,
        out_specs=[vm] * 4,
        scratch_shapes=scratch(),
        compiler_params=pltpu.CompilerParams(
            collective_id=0, has_side_effects=True, vmem_limit_bytes=62 * 2 ** 20),
        name="joint_block",
    )(
        img_tokens, txt_tokens, jnp.transpose(img_weight, (1, 0, 2)),
        jnp.transpose(txt_weight, (1, 0, 2)), img_modulation, txt_modulation, features,
        qk_gains.reshape(4, HD), valid_text, img_cotangent, txt_cotangent,
    )
    shapes = tuple(jax.ShapeDtypeStruct(v.shape, v.dtype) for v in (dw_img, dw_txt, dx_img, dx_txt))
    dw_img, dw_txt, dx_img, dx_txt = pl.pallas_call(
        finish, out_shape=shapes, in_specs=[vm] * 4, out_specs=[vm] * 4, name="results",
    )(dw_img, dw_txt, dx_img, dx_txt)
    return (
        jnp.transpose(dw_img, (1, 0, 2)), jnp.transpose(dw_txt, (1, 0, 2)), dx_img, dx_txt
    )


def solution(mesh):
    return jax.shard_map(
        on_device,
        mesh=mesh,
        in_specs=(
            P("seq", None),
            P("seq", None),
            P("fsdp", None, None),
            P("fsdp", None, None),
            P(),
            P(),
            P(),
            P(),
            P(),
            P("seq", "fsdp"),
            P("seq", "fsdp"),
        ),
        out_specs=(
            P("seq", None, "fsdp"),
            P("seq", None, "fsdp"),
            P("seq", "fsdp"),
            P("seq", "fsdp"),
        ),
        check_vma=False,
    )
```

time: 177 us -> 112 us (0.63)
  Pallas kernels: 165 us -> 109 us
  local copies, waits for them, and re-layouts: 9.52 us -> 0 us
    pallas_call x1, Pallas kernels: 165 us -> 107 us  [on_device(): pl.pallas_call(kernel, out_shape=(jax.ShapeDtypeStruct((3, 192, 256), F32...]
    unnamed x4 -> x0, local copies, waits for them, and re-layouts: 6.8 us -> none
    pallas_call x0 -> x1, Pallas kernels: none -> 2.39 us  [on_device(): pl.pallas_call(finish, out_shape=shapes, in_specs=[vm] * 4, out_specs=[vm...]
where the time goes in v4:
time: 112 us
  Pallas kernels  109 us (97%)
  between operations  1.94 us (2%)
    pallas_call x1, Pallas kernels, on_device(): pl.pallas_call(kernel, out_shape=(jax.ShapeDtypeStruct((3, 192, 256), F32...  107 us
    pallas_call x1, Pallas kernels, on_device(): pl.pallas_call(finish, out_shape=shapes, in_specs=[vm] * 4, out_specs=[vm...  2.39 us

profile of v4, /device:TPU:1, one launch (start us, length us, event | category | flops | bytes accessed | tf_op | source)
XLA Modules:
  0.0 111.5 jit_solution(7910529697811134250)
XLA Ops:
  2.0 0.6 fusion.feat
  2.6 106.5 %joint_block.1 = (f32[3,192,256]{2,1,0:T(8,128)}, f32[3,192,256]{2,1,0:T(8,128)}, bf16[256,384]{1,0:T(8,128)(2,1)}, bf16[32,384]{1,0:T(8,128)(2,1)}) custom-call(bf16[256,3072]{1,0:T(8,128)(2,1)} %x_img.1, bf16[32,3072]{1,0:T(8,128)(2,1)} %x_txt.1, bf16[3,384,2048]{2,1,0:T(8,128)(2,1)} %bitcast.10, bf16[3,384,2048]{2,1,0:T(8,128)(2,1)} %bitcast.11, ...), custom_call_target="tpu_custom_call" | custom-call | tf_op jit(solution)/shard_map/joint_block/pallas_call | solution.py:732
  109.1 2.4 %results.1 = (f32[3,192,256]{2,1,0:T(8,128)}, f32[3,192,256]{2,1,0:T(8,128)}, bf16[256,384]{1,0:T(8,128)(2,1)}, bf16[32,384]{1,0:T(8,128)(2,1)}) custom-call(f32[3,192,256]{2,1,0:T(8,128)} %get-tuple-element.12.a, f32[3,192,256]{2,1,0:T(8,128)} %get-tuple-element.13.b, bf16[256,384]{1,0:T(8,128)(2,1)} %get-tuple-element.14.c, ...), custom_call_target="tpu_custom_call" | custom-call | tf_op jit(solution)/shard_map/results/pallas_call | solution.py:752
  (1 shorter events, 0.0 us)

commit v5 on v4

--- a/solution.py
+++ b/solution.py
@@ -471,18 +471,17 @@
     def dw_block(a, b):
         return dot_tn(hid[chip_at(a * 4 + b, 1)], gq[128:, :])
 
-    def rl_copy(a, d):
+    def rl_copy(d):
         rows = pl.ds(d * 192, 192)
-        return remote(dws.at[a * 4 + 2, rows], rl.at[a, rows], rl_ss.at[a, d], rl_rs.at[a, d],
+        return remote(dws.at[2, rows], rl.at[0, rows], rl_ss.at[0, d], rl_rs.at[0, d],
                       sdev(1 + 2 * d, 1))
 
     def dw_copy(r):
         return remote(dws.at[r], dwr.at[r], dw_ss.at[r], dw_rs.at[r], sdev(r % 4, 1))
 
     dws[6] = dw_block(1, 2).astype(BF)
-    for d in (0, 1):
-        rl_copy(1, d).start()
-    dws[2] = dw_block(0, 2).astype(BF)
+    cp_rx = remote(dws.at[6], rl.at[1], x_ss.at[7], x_rs.at[7], xdev)
+    cp_rx.start()
 
     other_rows = pl.ds(pl.multiple_of(128 + o * 256, 128), 256)
 
@@ -495,10 +494,9 @@
         px_copy(r).start()
 
     loop(0, 8, partner_part)
-    for d in (0, 1):
-        rl_copy(1, d).wait_send()
-    for d in (0, 1):
-        rl_copy(0, d).start()
+    for r in (5, 7):
+        dws[r] = dw_block(1, r % 4).astype(BF)
+        dw_copy(r).start()
 
     def ph_copy(r):
         return remote(phs.at[r], phr.at[r], ph_ss.at[1, r], ph_rs.at[1, r], fdev(r % 4, -1))
@@ -522,37 +520,7 @@
         s1v[...] += t[:, 0:128] + t[:, 128:256] + t[:, 256:384]
         s2v[...] += u[:, 0:128] + u[:, 128:256] + u[:, 256:384]
 
-    def passed_on(a, d):
-        rl_copy(a, d).wait_recv()
-        r = a * 4 + 1 + 2 * d
-        block = dw_block(a, 1 + 2 * d)
-        lo, hi = d * 192, d * 192 + 192
-        dws[r, 192 - lo:384 - lo, :] = block[192 - lo:384 - lo].astype(BF)
-        dws[r, lo:hi, :] = (block[lo:hi] + rl[a, lo:hi, :].astype(F32)).astype(BF)
-
-    loop(0, 2, hidden_part)
-    for d in (0, 1):
-        passed_on(1, d)
-        dw_copy(5 + 2 * d).start()
-    loop(2, 6, hidden_part)
-    for d in (0, 1):
-        passed_on(0, d)
-    for d in (0, 1):
-        dw_copy(5 + 2 * d).wait_send()
-    for d in (0, 1):
-        dw_copy(1 + 2 * d).start()
-    loop(1, 8, lambda r: gs_copy(r).start())
-    loop(6, 8, hidden_part)
-
-    lane = lax.broadcasted_iota(jnp.int32, (256, 128), 1)
-    s1 = jnp.sum(s1v[...], axis=-1, keepdims=True)
-    s2 = jnp.sum(s2v[...], axis=-1, keepdims=True)
-    sts[...] = jnp.where(lane == 0, s1, s2).T[0:8]
-
-    def st_copy(r):
-        return remote(sts, str_.at[r], st_ss.at[r], st_rs.at[r], fdev(r, 1))
-
-    loop(1, 8, lambda r: st_copy(r).start())
+    loop(0, 4, hidden_part)
 
     thx[...] = jnp.zeros_like(thx)
 
@@ -568,20 +536,12 @@
     cp_th = remote(thx.at[their], thr, p_ss.at[4], p_rs.at[4], pdev)
     cp_th.start()
 
-    cp_th.wait_recv()
-    gh = thx[txt_rows, :] + thr[...]
-    tsc = gh * sc[0, f, 0:1, :]
-    tn = ntxt[f]
-    t1 = jnp.sum(tsc, axis=-1, keepdims=True)
-    t2 = jnp.sum(tsc * tn, axis=-1, keepdims=True)
-    lane_t = lax.broadcasted_iota(jnp.int32, (32, 128), 1)
-    tsts[...] = jnp.where(lane_t == 0, t1, t2)
-
-    def ts_copy(r):
-        return remote(tsts, tstr.at[r], ts_ss.at[r], ts_rs.at[r], fdev(r, 1))
-
-    loop(1, 8, lambda r: ts_copy(r).start())
-    thr[...] = tsc
+    wx[...] = dw_block(0, 2)
+    cp_rx.wait_recv()
+    dws[2] = (wx[...] + rl[1].astype(F32)).astype(BF)
+    for d in (0, 1):
+        rl_copy(d).start()
+    loop(1, 8, lambda r: gs_copy(r).start())
 
     mine = pl.ds(pl.multiple_of(c * 192, 64), 192)
     theirs = pl.ds(pl.multiple_of(o * 192, 64), 192)
@@ -594,6 +554,43 @@
     cp_wo = remote(wcs.at[theirs], wcr.at[1], x_ss.at[6], x_rs.at[6], xodev)
     cp_wc.start()
     cp_wo.start()
+
+    cp_th.wait_recv()
+    gh = thx[txt_rows, :] + thr[...]
+    tsc = gh * sc[0, f, 0:1, :]
+    tn = ntxt[f]
+    t1 = jnp.sum(tsc, axis=-1, keepdims=True)
+    t2 = jnp.sum(tsc * tn, axis=-1, keepdims=True)
+    lane_t = lax.broadcasted_iota(jnp.int32, (32, 128), 1)
+    tsts[...] = jnp.where(lane_t == 0, t1, t2)
+
+    def ts_copy(r):
+        return remote(tsts, tstr.at[r], ts_ss.at[r], ts_rs.at[r], fdev(r, 1))
+
+    loop(1, 8, lambda r: ts_copy(r).start())
+    thr[...] = tsc
+
+    loop(5, 8, lambda r: ph_copy(r).wait_send())
+    loop(4, 8, hidden_part)
+    lane = lax.broadcasted_iota(jnp.int32, (256, 128), 1)
+    s1 = jnp.sum(s1v[...], axis=-1, keepdims=True)
+    s2 = jnp.sum(s2v[...], axis=-1, keepdims=True)
+    sts[...] = jnp.where(lane == 0, s1, s2).T[0:8]
+
+    def st_copy(r):
+        return remote(sts, str_.at[r], st_ss.at[r], st_rs.at[r], fdev(r, 1))
+
+    loop(1, 8, lambda r: st_copy(r).start())
+
+    for d in (0, 1):
+        r = 1 + 2 * d
+        lo, hi = d * 192, d * 192 + 192
+        wx[...] = dw_block(0, r)
+        rl_copy(d).wait_recv()
+        dws[r, 192 - lo:384 - lo, :] = wx[192 - lo:384 - lo, :].astype(BF)
+        dws[r, lo:hi, :] = (wx[lo:hi, :] + rl[0, lo:hi, :].astype(F32)).astype(BF)
+        dw_copy(r).start()
+
     hsum = phs[4].astype(F32)
     for r in (5, 6, 7):
         ph_copy(r).wait_recv()
@@ -660,10 +657,6 @@
         for cp in (t_copy, h_copy, gf_copy, gs_copy, st_copy, ts_copy):
             cp(r).wait_send()
 
-        @pl.when(r % 4 != 0)
-        def _():
-            ph_copy(r).wait_send()
-
     def drain_z(b):
         for part in (0, 1):
             ring_copy(dO, do_ss, do_rs, part, b, z).wait_send()
@@ -674,11 +667,13 @@
     loop(1, 8, drain)
     loop(1, 4, drain_z)
     loop(0, 8, lambda r: px_copy(r).wait_send())
+    loop(1, 4, lambda r: ph_copy(r).wait_send())
     for d in (0, 1):
-        rl_copy(0, d).wait_send()
-        dw_copy(1 + 2 * d).wait_send()
+        rl_copy(d).wait_send()
+    for r in (1, 3, 5, 7):
+        dw_copy(r).wait_send()
     for cp in (cp_coti, cp_cott, cp_ht, cp_hi, cp_th, cp_wt, cp_wi, cp_kvk, cp_kvv, cp_kvt,
-               cp_dk, cp_wc, cp_wo, cp_hc):
+               cp_dk, cp_rx, cp_wc, cp_wo, cp_hc):
         cp.wait_send()
 
 
@@ -715,7 +710,7 @@
     ] + [
         pltpu.SemaphoreType.DMA(shape)
         for shape in (
-            [(6,), (3,), (8, 3), (8, 3), (8, 3), (2, 2, 8), (2, 2, 8), (7,), (7,), (7,), (7,)]
+            [(6,), (3,), (8, 3), (8, 3), (8, 3), (2, 2, 8), (2, 2, 8), (7,), (7,), (8,), (8,)]
             + [(8,)] * 4 + [(2, 4)] * 6 + [(4,)] * 2 + [(2, 2)] * 2 + [(8,)] * 6
             + [(2, 8)] * 2 + [(8,)] * 4
         )

time: 112 us -> 102 us (0.911)
  Pallas kernels: 109 us -> 99.7 us
    pallas_call x1, Pallas kernels: 107 us -> 97.3 us  [on_device(): pl.pallas_call(kernel, out_shape=(jax.ShapeDtypeStruct((3, 192, 256), F32...]
where the time goes in v5:
time: 102 us
  Pallas kernels  99.7 us (98%)
  between operations  1.94 us (2%)
    pallas_call x1, Pallas kernels, on_device(): pl.pallas_call(kernel, out_shape=(jax.ShapeDtypeStruct((3, 192, 256), F32...  97.3 us
    pallas_call x1, Pallas kernels, on_device(): pl.pallas_call(finish, out_shape=shapes, in_specs=[vm] * 4, out_specs=[vm...  2.39 us

profile of v5, /device:TPU:1, one launch (start us, length us, event | category | flops | bytes accessed | tf_op | source)
XLA Modules:
  0.0 102.3 jit_solution(9228602174660480852)
XLA Ops:
  2.0 0.6 fusion.feat
  2.6 97.3 %joint_block.1 = (f32[3,192,256]{2,1,0:T(8,128)}, f32[3,192,256]{2,1,0:T(8,128)}, bf16[256,384]{1,0:T(8,128)(2,1)}, bf16[32,384]{1,0:T(8,128)(2,1)}) custom-call(bf16[256,3072]{1,0:T(8,128)(2,1)} %x_img.1, bf16[32,3072]{1,0:T(8,128)(2,1)} %x_txt.1, bf16[3,384,2048]{2,1,0:T(8,128)(2,1)} %bitcast.10, bf16[3,384,2048]{2,1,0:T(8,128)(2,1)} %bitcast.11, ...), custom_call_target="tpu_custom_call" | custom-call | tf_op jit(solution)/shard_map/joint_block/pallas_call | solution.py:727
  99.9 2.4 %results.1 = (f32[3,192,256]{2,1,0:T(8,128)}, f32[3,192,256]{2,1,0:T(8,128)}, bf16[256,384]{1,0:T(8,128)(2,1)}, bf16[32,384]{1,0:T(8,128)(2,1)}) custom-call(f32[3,192,256]{2,1,0:T(8,128)} %get-tuple-element.12.a, f32[3,192,256]{2,1,0:T(8,128)} %get-tuple-element.13.b, bf16[256,384]{1,0:T(8,128)(2,1)} %get-tuple-element.14.c, ...), custom_call_target="tpu_custom_call" | custom-call | tf_op jit(solution)/shard_map/results/pallas_call | solution.py:747
  (1 shorter events, 0.0 us)

commit v6 on v5

--- a/solution.py
+++ b/solution.py
@@ -164,11 +164,14 @@
         loop(1, 8, one)
 
     def start_keys():
-        loop(1, 8, lambda r: w_copy(r, 0).wait_send())
         loop(1, 8, lambda r: w_copy(r, 1).start())
+
+    def start_values():
+        loop(1, 8, lambda r: wv_copy(r).start())
 
     pl.semaphore_wait(barrier, 16)
     loop(1, 8, lambda r: w_copy(r, 0).start())
+    start_keys()
     loop(0, 8, start_wt)
 
     img_rows = pl.ds(pl.multiple_of(128 + c * 256, 128), 256)
@@ -228,7 +231,7 @@
                 nrm[b, pl.ds(at, rows), :] = n[:, b * 384:(b + 1) * 384]
                 put(b, at, rows, h[:, b * 384:(b + 1) * 384])
             if which == 1:
-                pl.when(i == 8)(start_keys)
+                pl.when(i == 4)(start_values)
 
         loop(0, src.shape[0] // rows, body)
 
@@ -242,15 +245,6 @@
     prepare(0, xt, ntxt, invt, put_txt)
     cp_ht = remote(hidt.at[:, txt_rows], hidt.at[:, txt_rows], p_ss.at[2], p_rs.at[2], pdev)
     cp_ht.start()
-    loc[0].wait()
-    prepare(1, xi, nimg, invi, put_img)
-    cp_hi = remote(hid.at[:, half_rows], hid.at[:, half_rows], p_ss.at[3], p_rs.at[3], pdev)
-    cp_hi.start()
-
-    pass_w(0)
-    loop(1, 8, lambda r: w_copy(r, 1).wait_send())
-    loop(1, 8, lambda r: wv_copy(r).start())
-
     cp_ht.wait_recv()
 
     def t_copy(r):
@@ -270,6 +264,13 @@
             t_copy(r).start()
 
     loop(0, 8, txt_partial)
+    loc[0].wait()
+    prepare(1, xi, nimg, invi, put_img)
+    cp_hi = remote(hid.at[:, half_rows], hid.at[:, half_rows], p_ss.at[3], p_rs.at[3], pdev)
+    cp_hi.start()
+
+    pass_w(0)
+
     pass_w(1)
 
     def normed_head(lo, hi, col, g):
@@ -651,6 +652,8 @@
 
     def drain(r):
         wv_copy(r).wait_send()
+        w_copy(r, 0).wait_send()
+        w_copy(r, 1).wait_send()
         for j in (0, 1):
             for d in (0, 1):
                 z_copy(j, d, r, hz).wait_send()
@@ -677,11 +680,17 @@
         cp.wait_send()
 
 
-def finish(a, b, c, d, oa, ob, oc, od):
-    oa[...] = a[...]
-    ob[...] = b[...]
-    oc[...] = c[...]
-    od[...] = d[...]
+def finish(*refs):
+    ins, outs, bufs, isem, osem = refs[0:4], refs[4:8], refs[8:12], refs[12], refs[13]
+    fetch = [pltpu.make_async_copy(ins[i], bufs[i], isem.at[i]) for i in range(4)]
+    store = [pltpu.make_async_copy(bufs[i], outs[i], osem.at[i]) for i in range(4)]
+    for cp in fetch:
+        cp.start()
+    for i in range(4):
+        fetch[i].wait()
+        store[i].start()
+    for cp in store:
+        cp.wait()
 
 
 def scratch():
@@ -745,7 +754,9 @@
     )
     shapes = tuple(jax.ShapeDtypeStruct(v.shape, v.dtype) for v in (dw_img, dw_txt, dx_img, dx_txt))
     dw_img, dw_txt, dx_img, dx_txt = pl.pallas_call(
-        finish, out_shape=shapes, in_specs=[vm] * 4, out_specs=[vm] * 4, name="results",
+        finish, out_shape=shapes, in_specs=[anys] * 4, out_specs=[anys] * 4, name="results",
+        scratch_shapes=[pltpu.VMEM(v.shape, v.dtype) for v in shapes]
+        + [pltpu.SemaphoreType.DMA((4,))] * 2,
     )(dw_img, dw_txt, dx_img, dx_txt)
     return (
         jnp.transpose(dw_img, (1, 0, 2)), jnp.transpose(dw_txt, (1, 0, 2)), dx_img, dx_txt

time: 102 us -> 100 us (0.980)
  Pallas kernels: 99.7 us -> 97.7 us
    pallas_call x1, Pallas kernels: 97.3 us -> 95.5 us  [on_device(): pl.pallas_call(kernel, out_shape=(jax.ShapeDtypeStruct((3, 192, 256), F32...]
where the time goes in v6:
time: 100 us
  Pallas kernels  97.7 us (98%)
  between operations  1.94 us (2%)
    pallas_call x1, Pallas kernels, on_device(): pl.pallas_call(kernel, out_shape=(jax.ShapeDtypeStruct((3, 192, 256), F32...  95.5 us
    pallas_call x1, Pallas kernels, on_device(): pl.pallas_call(finish, out_shape=shapes, in_specs=[anys] * 4, out_specs=[...  2.2 us

profile of v6, /device:TPU:1, one launch (start us, length us, event | category | flops | bytes accessed | tf_op | source)
XLA Modules:
  0.0 100.3 jit_solution(14810768079810010244)
XLA Ops:
  2.0 0.6 fusion.feat
  2.6 95.5 %joint_block.1 = (f32[3,192,256]{2,1,0:T(8,128)}, f32[3,192,256]{2,1,0:T(8,128)}, bf16[256,384]{1,0:T(8,128)(2,1)}, bf16[32,384]{1,0:T(8,128)(2,1)}) custom-call(bf16[256,3072]{1,0:T(8,128)(2,1)} %x_img.1, bf16[32,3072]{1,0:T(8,128)(2,1)} %x_txt.1, bf16[3,384,2048]{2,1,0:T(8,128)(2,1)} %bitcast.10, bf16[3,384,2048]{2,1,0:T(8,128)(2,1)} %bitcast.11, ...), custom_call_target="tpu_custom_call" | custom-call | tf_op jit(solution)/shard_map/joint_block/pallas_call | solution.py:736
  98.1 2.2 %results.1 = (f32[3,192,256]{2,1,0:T(8,128)}, f32[3,192,256]{2,1,0:T(8,128)}, bf16[256,384]{1,0:T(8,128)(2,1)}, bf16[32,384]{1,0:T(8,128)(2,1)}) custom-call(f32[3,192,256]{2,1,0:T(8,128)} %get-tuple-element.12.refs_0_, f32[3,192,256]{2,1,0:T(8,128)} %get-tuple-element.13.refs_1_, bf16[256,384]{1,0:T(8,128)(2,1)} %get-tuple-element.14.refs_2_, ...), custom_call_target="tpu_custom_call" | custom-call | tf_op jit(solution)/shard_map/results/pallas_call | solution.py:756
  (1 shorter events, 0.0 us)
